TPU v7x, 128 devices: a whole 4x4x4 slice. The times are simulated.
128 devices in a mesh: pair: 16 (over y, x), ctr: 8 (over z, core).
Axes of the slice: x: 4, y: 4, z: 4, core: 2. Of those that a mesh axis runs over, the one named last changes fastest.
Arguments:
- amp_tiles: bfloat16 [32768, 9216], P(('pair', 'ctr')), may hold values from -6 to 6
- amp_rows: int32 [32768], P(('pair', 'ctr')), may hold values from 0 to 191, as said below
- amp_cols: int32 [32768], P(('pair', 'ctr')), may hold values from 0 to 191
- int_tiles: bfloat16 [8, 288, 9216], P('ctr', 'pair'), may hold values from -0.0625 to 0.0625
- int_rows: int32 [8, 288], P('ctr', 'pair'), may hold values from 0 to 191, as said below
- int_cols: int32 [8, 288], P('ctr', 'pair'), may hold values from 0 to 23
Outputs:
- cycle: bfloat16 [18432, 2304], P(('pair', 'ctr'))
Inputs may be any that keep to these rules, and one draw needn't show every extreme that they name: Together with amp_cols, no position is named twice. A tile's owner is the device with pair index amp_rows // 12 and ctr index amp_cols // 24. Each device holds at most 4 tiles of one owner, exactly that many for some owners in every draw, and every device owns exactly 256 tiles. int_rows[g, t] lies in g * 2 * 12 to (g + 1) * 2 * 12 - 1; no pair (int_rows, int_cols) is named twice.
All inputs are finite; a program needn't handle non-finite values.
Results may differ from a plain program's by a relative error of at most 0.017.
Values may be sent and summed in bfloat16 or wider, within the bound.
No kernel may reach another device: no remote copies, remote signals or barrier semaphores. Data moves between devices by JAX's collectives and lax.ppermute only.
A program may use at most 192 MiB of HBM per device.

v0:
```python
import jax
import jax.numpy as jnp
from jax import lax
from jax.sharding import PartitionSpec as P

TILE = 96
VT = 12
OI_DEV = 1
OK_DEV = 2
OJ = 2


def on_device(amp_tiles, amp_rows, amp_cols, int_tiles, int_rows, int_cols):
    pair_count = lax.axis_size("pair")
    ctr_count = lax.axis_size("ctr")
    devices = pair_count * ctr_count
    row_tiles = OI_DEV * VT
    ctr_tiles = OK_DEV * VT
    col_tiles = OJ * VT
    flat = amp_tiles.shape[1]
    held = amp_tiles.shape[0]
    capacity = 2 * held // devices
    target = amp_rows // row_tiles * ctr_count + amp_cols // ctr_tiles
    position = amp_cols % ctr_tiles * row_tiles + amp_rows % row_tiles
    onehot = (target[:, None] == jnp.arange(devices, dtype=jnp.int32)[None, :]).astype(jnp.int32)
    ranking = jnp.sum((jnp.cumsum(onehot, axis=0) - 1) * onehot, axis=1)
    landing = target * capacity + ranking
    outgoing = jnp.zeros((devices * capacity, flat), jnp.bfloat16).at[landing].set(amp_tiles)
    labels = jnp.full((devices * capacity,), -1, jnp.int32).at[landing].set(position)
    arrived, arrived_labels = (
        lax.all_to_all(outgoing, ("pair", "ctr"), split_axis=0, concat_axis=0, tiled=True),
        lax.all_to_all(labels, ("pair", "ctr"), split_axis=0, concat_axis=0, tiled=True),
    )
    cells = row_tiles * ctr_tiles
    targets = jnp.where(arrived_labels >= 0, arrived_labels, cells)
    placed = jnp.zeros((cells, flat), jnp.bfloat16).at[targets].set(arrived, mode="drop")
    amp_local = placed.reshape(ctr_tiles, row_tiles * TILE, TILE)
    ctr_base = lax.axis_index("ctr") * ctr_tiles
    rows_total = row_tiles * TILE
    empty = jnp.zeros((rows_total, col_tiles, TILE), jnp.float32)
    column_ids = jnp.arange(col_tiles, dtype=jnp.int32)
    total = empty
    piece_tiles = lax.all_gather(int_tiles, "pair", axis=1, tiled=True)
    piece_rows = lax.all_gather(int_rows, "pair", axis=1, tiled=True)
    piece_cols = lax.all_gather(int_cols, "pair", axis=1, tiled=True)
    length = piece_rows.shape[0] * piece_rows.shape[1]
    stride = max((part_size for part_size in range(1, 49) if length % part_size == 0))
    blocks = piece_tiles.reshape(length // stride, stride, TILE, TILE)
    block_rows = piece_rows.reshape(length // stride, stride) - ctr_base
    block_cols = piece_cols.reshape(length // stride, stride)

    def one_block(accum, item):
        weights, contract_idx, column_idx = item
        chosen = jnp.take(amp_local, contract_idx, axis=0)
        contrib = jnp.einsum("nrc,ncq->nrq", chosen, weights, preferred_element_type=jnp.float32)
        selector = (column_idx[:, None] == column_ids[None, :]).astype(jnp.float32)
        spread_sum = jnp.einsum(
            "nrq,nj->rjq",
            contrib,
            selector,
            precision=lax.Precision.HIGHEST,
            preferred_element_type=jnp.float32,
        )
        return (accum + spread_sum, None)

    total, unused = lax.scan(one_block, total, (blocks, block_rows, block_cols))
    partial_value = total
    partial_value = partial_value.reshape(rows_total, col_tiles * TILE)
    summed = lax.psum_scatter(
        partial_value.astype(jnp.bfloat16), "ctr", scatter_dimension=0, tiled=True
    )
    return summed


def solution(mesh):
    placed = (
        P(("pair", "ctr"), None),
        P(("pair", "ctr")),
        P(("pair", "ctr")),
        P("ctr", "pair", None),
        P("ctr", "pair"),
        P("ctr", "pair"),
    )
    return jax.shard_map(
        on_device, mesh=mesh, in_specs=placed, out_specs=P(("pair", "ctr"), None), check_vma=False
    )
```

profile of v0, /device:TPU:0, one launch (start us, length us, event | category | flops | bytes accessed | tf_op | source)
XLA Modules:
  0.0 746.4 jit_solution(11482455239910796938)
XLA Ops:
  12.4 11.1 %all-to-all-start = ((s32[128,4,1]{1,2,0:T(1,128)}), s32[128,4,1]{1,2,0:T(1,128)S(1)}, u32[]{:S(2)}, u32[]{:S(2)}) async-start(s32[128,4,1]{1,2,0:T(1,128)} %bitcast.7), calls=%async_computation | async-start | bytes 131072 | tf_op jit(solution)/shard_map/all_to_all | solution.py:32
  23.6 13.8 %scatter_custom_fusion.1 = bf16[512,9216]{1,0:T(8,128)(2,1)} fusion(s32[256]{0:T(256)S(1)} %compare_select_fusion.4, bf16[256,9216]{1,0:T(8,128)(2,1)} %param.8, bf16[]{:T(256)} %constant.78.clone.1), kind=kCustom, calls=%fused_computation.28 | custom fusion | bytes 9437696 | tf_op jit(solution)/shard_map/scatter | solution.py:28
  37.4 14.0 %all_to_all.19 = bf16[128,4,9216]{2,1,0:T(4,128)(2,1)} reshape(bf16[512,9216]{1,0:T(8,128)(2,1)} %scatter_custom_fusion.1) | data formatting | bytes 18874368 | tf_op jit(solution)/shard_map/all_to_all | solution.py:31
  51.4 10.2 %all-to-all-start.1 = ((bf16[128,4,9216]{2,1,0:T(4,128)(2,1)}), bf16[128,4,9216]{2,1,0:T(4,128)(2,1)}, u32[]{:S(2)}, u32[]{:S(2)}) async-start(bf16[128,4,9216]{2,1,0:T(4,128)(2,1)} %all_to_all.19), calls=%async_computation.1 | async-start | bytes 18874368 | tf_op jit(solution)/shard_map/all_to_all | solution.py:31
  63.0 144.5 %all-reduce.2 = (s32[288]{0:T(512)S(1)}, s32[288]{0:T(512)S(1)}) all-reduce(s32[288]{0:T(512)S(1)} %bitcast_dynamic-update-slice_fusion.1, s32[288]{0:T(512)S(1)} %bitcast_dynamic-update-slice_fusion), channel_id=1, replica_groups=mesh['pair'=16,'ctr'=8] {'pair'}, use_global_device_ids=true, to_apply=%add | all-reduce | flops 576 | bytes 4608
  209.0 13.1 %reshape.133 = bf16[512,9216]{1,0:T(8,128)(2,1)} reshape(bf16[128,4,9216]{2,1,0:T(4,128)(2,1)} %all-to-all-done.1) | data formatting | bytes 18874368 | tf_op jit(solution)/shard_map/all_to_all | solution.py:31
  222.1 19.5 %scatter_custom_fusion.2 = bf16[288,9216]{1,0:T(8,128)(2,1)} fusion(s32[512]{0:T(512)S(1)} %bitcast.52, bf16[512,9216]{1,0:T(8,128)(2,1)} %reshape.133, bf16[]{:T(256)} %constant.78.clone.1), kind=kCustom, calls=%fused_computation.30 | custom fusion | bytes 5308928 | tf_op jit(solution)/shard_map/scatter | solution.py:36
  241.6 11.3 %reshape.103 = bf16[24,1152,96]{2,1,0:T(8,128)(2,1)} reshape(bf16[288,9216]{1,0:T(8,128)(2,1)} %scatter_custom_fusion.2) | data formatting | bytes 10616832 | tf_op jit(solution)/shard_map/reshape | solution.py:37
  252.8 114.2 %reduce = bf16[288,9216]{1,0:T(8,128)(2,1)} reduce(bf16[1,288,9216]{2,0,1:T(2,128)(2,1)} %all-gather.2.cloned.1.call-done, bf16[]{:T(256)} %constant.101), dimensions={0}, to_apply=%all_gather.11.reduce_sub_computation | reduce | bytes 10616834 | tf_op jit(solution)/shard_map/all_gather | solution.py:43
  367.1 11.2 %reshape.104 = bf16[6,48,96,96]{3,2,1,0:T(8,128)(2,1)} reshape(bf16[288,9216]{1,0:T(8,128)(2,1)} %reduce) | data formatting | bytes 10616832 | tf_op jit(solution)/shard_map/reshape | solution.py:48
  378.3 305.5 %while.11 = (s32[]{:T(128)}, f32[1152,24,96]{0,1,2:T(8,128)}, s32[6,48]{1,0:T(8,128)S(1)}, s32[6,48]{1,0:T(8,128)S(1)}, bf16[24,1152,96]{2,1,0:T(8,128)(2,1)}, /...) while((s32[]{:T(128)}, f32[1152,24,96]{0,1,2:T(8,128)}, s32[6,48]{1,0:T(8,128)S(1)}, ...), condition=%wide.region_7.8_spmd.clone, body=%wide.region_6.7_spmd.clone.sunk | while | flops 2558659072 | bytes 100276424 | solution.py:66
  378.3 9.9 %gather_fusion = bf16[48,1152,96]{2,1,0:T(8,128)(2,1)} fusion(bf16[24,1152,96]{2,1,0:T(8,128)(2,1)} %get-tuple-element.151, s32[1024]{0:T(1024)S(1)} %pad_clamp_fusion.2), kind=kCustom, calls=%fused_computation.clone.clone.1 | custom fusion | bytes 21233856 | tf_op jit(solution)/shard_map/while/body/eval_jaxpr/jit(_take)/gather | solution.py:54
  388.2 12.9 %fusion.44 = f32[48,1152,96]{1,2,0:T(8,128)} fusion(bf16[48,1152,96]{2,1,0:T(8,128)(2,1)} %gather_fusion, pred[48]{0:T(512)(128)(4,1)S(1)} %compare_and_fusion.2, bf16[6,48,96,96]{3,2,1,0:T(8,128)(2,1)} %get-tuple-element.152, s32[]{:T(128)} %get-tuple-element.139), kind=kOutput, calls=%fused_computation.7.clone.1 | convolution fusion | flops 1024524288 | bytes 36569648 | tf_op jit(solution)/shard_map/while/body/eval_jaxpr/nrc,ncq->nrq/dot_general | solution.py:55
  401.1 27.1 %bitcast_add_fusion.2 = f32[1152,24,96]{0,1,2:T(8,128)} fusion(f32[1152,24,96]{0,1,2:T(8,128)} %get-tuple-element.140, f32[48,1152,96]{1,2,0:T(8,128)} %fusion.44, pred[]{:T(512)S(6)} %compare.3, s32[48]{0:T(128)S(1)} %fusion.45), kind=kOutput, calls=%fused_computation.10.clone.1 | convolution fusion | flops 1534133376 | bytes 42467520 | tf_op jit(solution)/shard_map/while/body/eval_jaxpr/nrq,nj->rjq/dot_general | solution.py:57
  428.2 9.9 %gather_fusion = bf16[48,1152,96]{2,1,0:T(8,128)(2,1)} fusion(bf16[24,1152,96]{2,1,0:T(8,128)(2,1)} %get-tuple-element.151, s32[1024]{0:T(1024)S(1)} %pad_clamp_fusion.2), kind=kCustom, calls=%fused_computation.clone.clone.1 | custom fusion | bytes 21233856 | tf_op jit(solution)/shard_map/while/body/eval_jaxpr/jit(_take)/gather | solution.py:54
  438.1 12.9 %fusion.44 = f32[48,1152,96]{1,2,0:T(8,128)} fusion(bf16[48,1152,96]{2,1,0:T(8,128)(2,1)} %gather_fusion, pred[48]{0:T(512)(128)(4,1)S(1)} %compare_and_fusion.2, bf16[6,48,96,96]{3,2,1,0:T(8,128)(2,1)} %get-tuple-element.152, s32[]{:T(128)} %get-tuple-element.139), kind=kOutput, calls=%fused_computation.7.clone.1 | convolution fusion | flops 1024524288 | bytes 36569648 | tf_op jit(solution)/shard_map/while/body/eval_jaxpr/nrc,ncq->nrq/dot_general | solution.py:55
  451.0 28.3 %bitcast_add_fusion.2 = f32[1152,24,96]{0,1,2:T(8,128)} fusion(f32[1152,24,96]{0,1,2:T(8,128)} %get-tuple-element.140, f32[48,1152,96]{1,2,0:T(8,128)} %fusion.44, pred[]{:T(512)S(6)} %compare.3, s32[48]{0:T(128)S(1)} %fusion.45), kind=kOutput, calls=%fused_computation.10.clone.1 | convolution fusion | flops 1534133376 | bytes 42467520 | tf_op jit(solution)/shard_map/while/body/eval_jaxpr/nrq,nj->rjq/dot_general | solution.py:57
  479.4 9.8 %gather_fusion = bf16[48,1152,96]{2,1,0:T(8,128)(2,1)} fusion(bf16[24,1152,96]{2,1,0:T(8,128)(2,1)} %get-tuple-element.151, s32[1024]{0:T(1024)S(1)} %pad_clamp_fusion.2), kind=kCustom, calls=%fused_computation.clone.clone.1 | custom fusion | bytes 21233856 | tf_op jit(solution)/shard_map/while/body/eval_jaxpr/jit(_take)/gather | solution.py:54
  489.2 12.9 %fusion.44 = f32[48,1152,96]{1,2,0:T(8,128)} fusion(bf16[48,1152,96]{2,1,0:T(8,128)(2,1)} %gather_fusion, pred[48]{0:T(512)(128)(4,1)S(1)} %compare_and_fusion.2, bf16[6,48,96,96]{3,2,1,0:T(8,128)(2,1)} %get-tuple-element.152, s32[]{:T(128)} %get-tuple-element.139), kind=kOutput, calls=%fused_computation.7.clone.1 | convolution fusion | flops 1024524288 | bytes 36569648 | tf_op jit(solution)/shard_map/while/body/eval_jaxpr/nrc,ncq->nrq/dot_general | solution.py:55
  502.1 28.3 %bitcast_add_fusion.2 = f32[1152,24,96]{0,1,2:T(8,128)} fusion(f32[1152,24,96]{0,1,2:T(8,128)} %get-tuple-element.140, f32[48,1152,96]{1,2,0:T(8,128)} %fusion.44, pred[]{:T(512)S(6)} %compare.3, s32[48]{0:T(128)S(1)} %fusion.45), kind=kOutput, calls=%fused_computation.10.clone.1 | convolution fusion | flops 1534133376 | bytes 42467520 | tf_op jit(solution)/shard_map/while/body/eval_jaxpr/nrq,nj->rjq/dot_general | solution.py:57
  530.5 9.9 %gather_fusion = bf16[48,1152,96]{2,1,0:T(8,128)(2,1)} fusion(bf16[24,1152,96]{2,1,0:T(8,128)(2,1)} %get-tuple-element.151, s32[1024]{0:T(1024)S(1)} %pad_clamp_fusion.2), kind=kCustom, calls=%fused_computation.clone.clone.1 | custom fusion | bytes 21233856 | tf_op jit(solution)/shard_map/while/body/eval_jaxpr/jit(_take)/gather | solution.py:54
  540.4 12.9 %fusion.44 = f32[48,1152,96]{1,2,0:T(8,128)} fusion(bf16[48,1152,96]{2,1,0:T(8,128)(2,1)} %gather_fusion, pred[48]{0:T(512)(128)(4,1)S(1)} %compare_and_fusion.2, bf16[6,48,96,96]{3,2,1,0:T(8,128)(2,1)} %get-tuple-element.152, s32[]{:T(128)} %get-tuple-element.139), kind=kOutput, calls=%fused_computation.7.clone.1 | convolution fusion | flops 1024524288 | bytes 36569648 | tf_op jit(solution)/shard_map/while/body/eval_jaxpr/nrc,ncq->nrq/dot_general | solution.py:55
  553.3 28.3 %bitcast_add_fusion.2 = f32[1152,24,96]{0,1,2:T(8,128)} fusion(f32[1152,24,96]{0,1,2:T(8,128)} %get-tuple-element.140, f32[48,1152,96]{1,2,0:T(8,128)} %fusion.44, pred[]{:T(512)S(6)} %compare.3, s32[48]{0:T(128)S(1)} %fusion.45), kind=kOutput, calls=%fused_computation.10.clone.1 | convolution fusion | flops 1534133376 | bytes 42467520 | tf_op jit(solution)/shard_map/while/body/eval_jaxpr/nrq,nj->rjq/dot_general | solution.py:57
  581.6 9.8 %gather_fusion = bf16[48,1152,96]{2,1,0:T(8,128)(2,1)} fusion(bf16[24,1152,96]{2,1,0:T(8,128)(2,1)} %get-tuple-element.151, s32[1024]{0:T(1024)S(1)} %pad_clamp_fusion.2), kind=kCustom, calls=%fused_computation.clone.clone.1 | custom fusion | bytes 21233856 | tf_op jit(solution)/shard_map/while/body/eval_jaxpr/jit(_take)/gather | solution.py:54
  591.5 12.8 %fusion.44 = f32[48,1152,96]{1,2,0:T(8,128)} fusion(bf16[48,1152,96]{2,1,0:T(8,128)(2,1)} %gather_fusion, pred[48]{0:T(512)(128)(4,1)S(1)} %compare_and_fusion.2, bf16[6,48,96,96]{3,2,1,0:T(8,128)(2,1)} %get-tuple-element.152, s32[]{:T(128)} %get-tuple-element.139), kind=kOutput, calls=%fused_computation.7.clone.1 | convolution fusion | flops 1024524288 | bytes 36569648 | tf_op jit(solution)/shard_map/while/body/eval_jaxpr/nrc,ncq->nrq/dot_general | solution.py:55
  604.3 28.4 %bitcast_add_fusion.2 = f32[1152,24,96]{0,1,2:T(8,128)} fusion(f32[1152,24,96]{0,1,2:T(8,128)} %get-tuple-element.140, f32[48,1152,96]{1,2,0:T(8,128)} %fusion.44, pred[]{:T(512)S(6)} %compare.3, s32[48]{0:T(128)S(1)} %fusion.45), kind=kOutput, calls=%fused_computation.10.clone.1 | convolution fusion | flops 1534133376 | bytes 42467520 | tf_op jit(solution)/shard_map/while/body/eval_jaxpr/nrq,nj->rjq/dot_general | solution.py:57
  632.7 9.9 %gather_fusion = bf16[48,1152,96]{2,1,0:T(8,128)(2,1)} fusion(bf16[24,1152,96]{2,1,0:T(8,128)(2,1)} %get-tuple-element.151, s32[1024]{0:T(1024)S(1)} %pad_clamp_fusion.2), kind=kCustom, calls=%fused_computation.clone.clone.1 | custom fusion | bytes 21233856 | tf_op jit(solution)/shard_map/while/body/eval_jaxpr/jit(_take)/gather | solution.py:54
  642.6 12.9 %fusion.44 = f32[48,1152,96]{1,2,0:T(8,128)} fusion(bf16[48,1152,96]{2,1,0:T(8,128)(2,1)} %gather_fusion, pred[48]{0:T(512)(128)(4,1)S(1)} %compare_and_fusion.2, bf16[6,48,96,96]{3,2,1,0:T(8,128)(2,1)} %get-tuple-element.152, s32[]{:T(128)} %get-tuple-element.139), kind=kOutput, calls=%fused_computation.7.clone.1 | convolution fusion | flops 1024524288 | bytes 36569648 | tf_op jit(solution)/shard_map/while/body/eval_jaxpr/nrc,ncq->nrq/dot_general | solution.py:55
  655.5 28.3 %bitcast_add_fusion.2 = f32[1152,24,96]{0,1,2:T(8,128)} fusion(f32[1152,24,96]{0,1,2:T(8,128)} %get-tuple-element.140, f32[48,1152,96]{1,2,0:T(8,128)} %fusion.44, pred[]{:T(512)S(6)} %compare.3, s32[48]{0:T(128)S(1)} %fusion.45), kind=kOutput, calls=%fused_computation.10.clone.1 | convolution fusion | flops 1534133376 | bytes 42467520 | tf_op jit(solution)/shard_map/while/body/eval_jaxpr/nrq,nj->rjq/dot_general | solution.py:57
  683.8 7.9 %copy.39 = bf16[1152,24,96]{0,2,1:T(8,128)(2,1)} copy(f32[1152,24,96]{0,1,2:T(8,128)} %get-tuple-element.42) | data formatting | bytes 15925248 | tf_op jit(solution)/shard_map/while | solution.py:66
  691.8 8.5 %copy.31 = bf16[1152,2304]{1,0:T(8,128)(2,1)} copy(bf16[1152,2304]{0,1:T(8,128)(2,1)} %bitcast.50) | data formatting | bytes 10616832
  700.3 39.0 %reduce-scatter.4.cloned.1.call-done = bf16[144,2304]{1,0:T(8,128)(2,1)} async-done(((bf16[1152,2304]{1,0:T(8,128)(2,1)}), bf16[144,2304]{1,0:T(8,128)(2,1)}) %reduce-scatter.4.cloned.1.call-update) | async-done | bytes 663568 | tf_op jit(solution)/shard_map/reduce_scatter | solution.py:69
  (63 shorter events, 8.3 us)
Async XLA Ops:
  6.5 246.3 %all-gather.2.cloned.1.call-start = ((), (), s32[]{:S(2)}) async-start(), calls=%async_computation.3 | async-start | bytes 11280384 | tf_op jit(solution)/shard_map/all_gather | solution.py:43
  12.4 38.9 %all-to-all-start = ((s32[128,4,1]{1,2,0:T(1,128)}), s32[128,4,1]{1,2,0:T(1,128)S(1)}, u32[]{:S(2)}, u32[]{:S(2)}) async-start(s32[128,4,1]{1,2,0:T(1,128)} %bitcast.7), calls=%async_computation | async-start | bytes 131072 | tf_op jit(solution)/shard_map/all_to_all | solution.py:32
  51.3 10.3 %copy-start.2 = (u32[128]{0:T(128)S(1)}, u32[128]{0:T(128)}, u32[]{:S(2)}) copy-start(u32[128]{0:T(128)} %constant.91) | copy-start | bytes 1540
  51.3 11.5 %copy-start = (s32[1,18]{1,0:T(1,128)S(1)}, s32[1,18]{1,0:T(1,128)}, u32[]{:S(2)}) copy-start(s32[1,18]{1,0:T(1,128)} %param.12) | copy-start | bytes 220
  51.3 11.6 %copy-start.1 = (s32[1,18]{1,0:T(1,128)S(1)}, s32[1,18]{1,0:T(1,128)}, u32[]{:S(2)}) copy-start(s32[1,18]{1,0:T(1,128)} %param.13) | copy-start | bytes 220
  51.4 157.6 %all-to-all-start.1 = ((bf16[128,4,9216]{2,1,0:T(4,128)(2,1)}), bf16[128,4,9216]{2,1,0:T(4,128)(2,1)}, u32[]{:S(2)}, u32[]{:S(2)}) async-start(bf16[128,4,9216]{2,1,0:T(4,128)(2,1)} %all_to_all.19), calls=%async_computation.1 | async-start | bytes 18874368 | tf_op jit(solution)/shard_map/all_to_all | solution.py:31
  61.6 677.8 %reduce-scatter.4.cloned.1.call-start = ((), (), s32[]{:S(2)}) async-start(), calls=%async_computation.4 | async-start | bytes 5971968 | tf_op jit(solution)/shard_map/reduce_scatter | solution.py:69
Sparse Core Ops, SparseCore 0:
  9.5 180.2 all-gather.1
  700.4 38.8 reduce-scatter.3
where the time goes:
time: 756 us; the launch traced here: 746 us
  matrix products  246 us (33%)
  local copies, waits for them, and re-layouts  165 us (22%)
  blocking collectives  144 us (19%)
  other arithmetic  116 us (15%)
  waiting for transfers between devices  39.1 us (5%)
  starting transfers between devices  21.4 us (3%)
  between operations  14.3 us (2%)
    dot_general x6, matrix products, one_block(): jnp.einsum('nrq,nj->rjq', contrib, selector, precision=lax.Precision.HIGH...  169 us
    unnamed x1, blocking collectives  144 us
    all_gather x1, other arithmetic, on_device(): piece_tiles = lax.all_gather(int_tiles, 'pair', axis=1, tiled=True)  114 us
    dot_general x6, matrix products, one_block(): jnp.einsum('nrc,ncq->nrq', chosen, weights, preferred_element_type=jnp.fl...  77.3 us
    gather x6, local copies, waits for them, and re-layouts, one_block(): chosen = jnp.take(amp_local, contract_idx, axis=0)  59.1 us
    reduce_scatter x1, waiting for transfers between devices, on_device(): lax.psum_scatter(partial_value.astype(jnp.bfloat16), 'ctr', scatter_dimen...  39 us
    all_to_all x2, local copies, waits for them, and re-layouts, on_device(): lax.all_to_all(outgoing, ('pair', 'ctr'), split_axis=0, concat_axis=0, ti...  27.1 us
    scatter x1, local copies, waits for them, and re-layouts, on_device(): jnp.zeros((cells, flat), jnp.bfloat16).at[targets].set(arrived, mode='drop')  19.5 us
  transfers between devices with their start and end apart: 4, of which 1 were waited for; matrix products, arithmetic and copies ran while one was open for 8% of the time, Pallas kernels for 0%

commit v1 on v0

v1 whole, which is shorter than its diff:
```python
import jax
import jax.numpy as jnp
from jax import lax
from jax.experimental import pallas as pl
from jax.experimental.pallas import tpu as pltpu
from jax.sharding import PartitionSpec as P

TILE = 96
VT = 12
KT = 24
JT = 24
FLAT = TILE * TILE
HALF = FLAT // 2
QUARTER = FLAT // 4
SLOTS = 4
LANES = 128
MIB = 2**20


def quad_unpack(v0, v1, v2, lane):
    return (v0, jnp.where(lane >= 96, v0, v1), jnp.where(lane >= 64, v1, v2), v2)


def turn(x, amount):
    amount = amount % LANES
    return x if amount == 0 else pltpu.roll(x, amount, 1)


def pack_kernel(land_ref, lab_ref, low_ref, high_ref, out_ref, first, second):
    step = pl.program_id(0)
    rows = first.shape[0]

    @pl.when(step == 0)
    def _():
        row = lax.broadcasted_iota(jnp.int32, first.shape, 0)
        land = jnp.broadcast_to(land_ref[...], first.shape)
        first[...] = jnp.where(row == land, 1.0, 0.0).astype(jnp.bfloat16)
        second[...] = jnp.where((row ^ SLOTS) == land, 1.0, 0.0).astype(jnp.bfloat16)

    def spread(low, high):
        a = jnp.dot(first[...], low, preferred_element_type=jnp.float32)
        b = jnp.dot(second[...], high, preferred_element_type=jnp.float32)
        n = a.shape[1]
        a = a.reshape(rows // 8, 1, 8, n)
        b = b.reshape(rows // 8, 1, 8, n)
        top = lax.broadcasted_iota(jnp.int32, a.shape, 2) < SLOTS
        both = jnp.concatenate([jnp.where(top, a, b), jnp.where(top, b, a)], axis=1)
        return both.reshape(rows * 2, n).astype(jnp.bfloat16)

    @pl.when(step < pl.num_programs(0) - 1)
    def _():
        out_ref[...] = spread(low_ref[...], high_ref[...])

    @pl.when(step == pl.num_programs(0) - 1)
    def _():
        out_ref[:, :LANES] = spread(lab_ref[...], lab_ref[...])


def pack(land, labels, tiles, devices):
    held = tiles.shape[0]
    block = 512
    steps = HALF // block
    return pl.pallas_call(
        pack_kernel,
        grid=(steps + 1,),
        out_shape=jax.ShapeDtypeStruct((devices * 2 * SLOTS, HALF + LANES), jnp.bfloat16),
        in_specs=[
            pl.BlockSpec((1, held), lambda s: (0, 0)),
            pl.BlockSpec((held, LANES), lambda s: (0, 0)),
            pl.BlockSpec((held, block), lambda s: (0, jnp.minimum(s, steps - 1))),
            pl.BlockSpec((held, block), lambda s: (0, steps + jnp.minimum(s, steps - 1))),
        ],
        out_specs=pl.BlockSpec((devices * 2 * SLOTS, block), lambda s: (0, s)),
        scratch_shapes=[pltpu.VMEM((devices * SLOTS, held), jnp.bfloat16)] * 2,
        compiler_params=pltpu.CompilerParams(vmem_limit_bytes=40 * MIB),
        name="pack",
    )(land, labels, tiles, tiles)


def label_rows(lab):
    unit = (
        lax.broadcasted_iota(jnp.int32, (8, LANES), 0)
        == lax.broadcasted_iota(jnp.int32, (8, LANES), 1)
    )
    return lax.dot_general(
        jnp.where(unit, 1.0, 0.0).astype(jnp.bfloat16),
        lab,
        (((1,), (1,)), ((), ())),
        preferred_element_type=jnp.float32,
    )


def integral_kernel(lab_ref, tiles_ref, out_ref, spread):
    quad = pl.program_id(0)
    labels = label_rows(lab_ref[...])
    cell = (labels[0:1] * 4 + labels[1:2] * (4 * KT) + labels[2:3]).astype(jnp.int32)
    shape = (4 * 4 * KT, lab_ref.shape[0])
    row = lax.broadcasted_iota(jnp.int32, shape, 0) + quad * (4 * 4 * KT)
    choose = jnp.where(row == jnp.broadcast_to(cell, shape), 1.0, 0.0).astype(jnp.bfloat16)
    for group in range(QUARTER // 384):
        block = jnp.dot(
            choose, tiles_ref[:, group * 384 : (group + 1) * 384], preferred_element_type=jnp.float32
        )
        lane = lax.broadcasted_iota(jnp.int32, (shape[0], LANES), 1)
        pieces = quad_unpack(block[:, :128], block[:, 128:256], block[:, 256:], lane)
        for a in range(4):
            for b in range(4):
                spread[b, pl.ds(group * 4 + a, 4 * KT, stride=24), :] = turn(
                    pieces[a][b * 96 : (b + 1) * 96], 32 * (a - b)
                )
    for part in range(KT):
        at = slice(part * 96, (part + 1) * 96)
        w = [spread[b, at, :] for b in range(4)]
        lane = lax.broadcasted_iota(jnp.int32, (96, LANES), 1)
        out_ref[at, 0:128] = jnp.where(lane < 96, w[0], w[1]).astype(jnp.bfloat16)
        out_ref[at, 128:256] = jnp.where(lane < 64, w[1], w[2]).astype(jnp.bfloat16)
        out_ref[at, 256:384] = jnp.where(lane < 32, w[2], w[3]).astype(jnp.bfloat16)


def place_integrals(gathered):
    rows = gathered.shape[0]
    return pl.pallas_call(
        integral_kernel,
        grid=(JT // 4,),
        out_shape=jax.ShapeDtypeStruct((KT * TILE, JT * TILE), jnp.bfloat16),
        in_specs=[
            pl.BlockSpec((rows, LANES), lambda s: (0, QUARTER // LANES)),
            pl.BlockSpec((rows, QUARTER), lambda s: (0, 0)),
        ],
        out_specs=pl.BlockSpec((KT * TILE, 4 * TILE), lambda s: (0, s)),
        scratch_shapes=[pltpu.VMEM((4, KT * TILE, LANES), jnp.float32)],
        compiler_params=pltpu.CompilerParams(vmem_limit_bytes=40 * MIB),
        name="integrals",
    )(gathered, gathered)


def product_kernel(odd_ref, lab_ref, low_ref, high_ref, b_ref, out_ref, choose, amp, total):
    step = pl.program_id(0)
    groups = QUARTER // 384

    @pl.when(step == 0)
    def _():
        labels = label_rows(lab_ref[...])
        column = lax.broadcasted_iota(jnp.int32, (1, lab_ref.shape[0]), 1)
        second = ((column & SLOTS) // SLOTS) ^ odd_ref[0]
        k = labels[0:1].astype(jnp.int32) - 1
        i = labels[1:2].astype(jnp.int32)
        cell = k * (2 * VT) + second * VT + i
        row = lax.broadcasted_iota(jnp.int32, choose.shape, 0)
        choose[...] = jnp.where(row == jnp.broadcast_to(cell, choose.shape), 1.0, 0.0).astype(
            jnp.bfloat16
        )

    @pl.when(step < groups)
    def _():
        low = jnp.dot(choose[...], low_ref[...], preferred_element_type=jnp.float32)
        high = jnp.dot(choose[...], high_ref[...], preferred_element_type=jnp.float32)
        lane = lax.broadcasted_iota(jnp.int32, (48, LANES), 1)
        for quad in range(KT // 4):
            pieces = []
            for b in range(4):
                at = slice((quad * 4 + b) * 24, (quad * 4 + b + 1) * 24)
                both = jnp.concatenate([low[at], high[at]], axis=0)
                pieces.append(quad_unpack(both[:, :128], both[:, 128:256], both[:, 256:], lane))
            for a in range(4):
                w = [turn(pieces[b][a], 32 * (a - b)) for b in range(4)]
                at = pl.ds(pl.multiple_of((step * 4 + a) * 48, 16), 48)
                base = quad * 384
                amp[at, base : base + 128] = jnp.where(lane < 96, w[0], w[1]).astype(jnp.bfloat16)
                amp[at, base + 128 : base + 256] = jnp.where(lane < 64, w[1], w[2]).astype(jnp.bfloat16)
                amp[at, base + 256 : base + 384] = jnp.where(lane < 32, w[2], w[3]).astype(jnp.bfloat16)

    @pl.when(step >= groups)
    def _():
        value = jnp.dot(amp[...], b_ref[...], preferred_element_type=jnp.float32)
        for part in range(total.shape[0]):
            lanes = slice(part * LANES, (part + 1) * LANES)
            total[part] = value[:, lanes]
            for i in range(VT):
                for h in range(2):
                    x = h * VT + i
                    rows = [total[part, pl.ds(x + 24 * q, 24, stride=48), :] for q in range(2)]
                    at = i * 96 + h * 48
                    out_ref[at : at + 48, lanes] = jnp.concatenate(rows, axis=0).astype(jnp.bfloat16)


def product(odd, arrived, integrals):
    groups = QUARTER // 384
    block = 256
    steps = integrals.shape[1] // block
    rows = arrived.shape[0]
    early = lambda s: jnp.minimum(s, groups - 1)
    late = lambda s: jnp.maximum(s - groups, 0)
    return pl.pallas_call(
        product_kernel,
        grid=(groups + steps,),
        out_shape=jax.ShapeDtypeStruct((VT * TILE, JT * TILE), jnp.bfloat16),
        in_specs=[
            pl.BlockSpec(memory_space=pltpu.SMEM),
            pl.BlockSpec((rows, LANES), lambda s: (0, HALF // LANES)),
            pl.BlockSpec((rows, 384), lambda s: (0, early(s))),
            pl.BlockSpec((rows, 384), lambda s: (0, groups + early(s))),
            pl.BlockSpec((KT * TILE, block), lambda s: (0, late(s))),
        ],
        out_specs=pl.BlockSpec((VT * TILE, block), lambda s: (0, late(s))),
        scratch_shapes=[
            pltpu.VMEM((2 * VT * KT, rows), jnp.bfloat16),
            pltpu.VMEM((VT * TILE, KT * TILE), jnp.bfloat16),
            pltpu.VMEM((block // LANES, VT * TILE, LANES), jnp.float32),
        ],
        compiler_params=pltpu.CompilerParams(vmem_limit_bytes=48 * MIB),
        name="product",
    )(odd, arrived, arrived, arrived, integrals)


def lanes_of(columns):
    stacked = jnp.stack(columns, axis=1).astype(jnp.bfloat16)
    return jnp.pad(stacked, ((0, 0), (0, LANES - stacked.shape[1])))


def on_device(amp_tiles, amp_rows, amp_cols, int_tiles, int_rows, int_cols):
    ctr_count = lax.axis_size("ctr")
    devices = lax.axis_size("pair") * ctr_count
    held = amp_tiles.shape[0]
    quarters = int_tiles[0].reshape(-1, 4, QUARTER).transpose(1, 0, 2).reshape(-1, QUARTER)
    four = jnp.repeat(jnp.arange(4, dtype=jnp.int32), int_rows.shape[1])
    int_labels = lanes_of([jnp.tile(int_rows[0] % KT, 4), jnp.tile(int_cols[0], 4), four])
    piece = jnp.concatenate([quarters, int_labels], axis=1)
    gathered = lax.all_gather(piece, "pair", axis=0, tiled=True)
    target = amp_rows // VT * ctr_count + amp_cols // KT
    order = jnp.arange(held, dtype=jnp.int32)
    earlier = (target[:, None] == target[None, :]) & (order[:, None] < order[None, :])
    land = target * SLOTS + jnp.sum(earlier.astype(jnp.int32), axis=0)
    labels = lanes_of([amp_cols % KT + 1, amp_rows % VT])
    outgoing = pack(land[None, :], labels, amp_tiles, devices)
    arrived = lax.all_to_all(outgoing, ("pair", "ctr"), split_axis=0, concat_axis=0, tiled=True)
    integrals = place_integrals(gathered)
    odd = (lax.axis_index("ctr") % 2).astype(jnp.int32).reshape(1)
    partial_value = product(odd, arrived, integrals)
    return lax.psum_scatter(partial_value, "ctr", scatter_dimension=0, tiled=True)


def solution(mesh):
    placed = (
        P(("pair", "ctr"), None),
        P(("pair", "ctr")),
        P(("pair", "ctr")),
        P("ctr", "pair", None),
        P("ctr", "pair"),
        P("ctr", "pair"),
    )
    return jax.shard_map(
        on_device, mesh=mesh, in_specs=placed, out_specs=P(("pair", "ctr"), None), check_vma=False
    )
```

time: 756 us -> 276 us (0.37); the launches traced: 746 us -> 276 us
  matrix products: 246 us -> 0 us
  local copies, waits for them, and re-layouts: 165 us -> 12.8 us
  blocking collectives: 144 us -> 0 us
  waiting for transfers between devices: 39.1 us -> 175 us
  other arithmetic: 116 us -> 2.96 us
  Pallas kernels: 0 us -> 60.3 us
  starting transfers between devices: 21.4 us -> 11.7 us
    dot_general x12 -> x0, matrix products: 246 us -> none  [the longest x6 169 us: one_block(): jnp.einsum('nrq,nj->rjq', contrib, selector, precision=lax.Precision.HIGH...]
    unnamed x1 -> x0, blocking collectives: 144 us -> none
    all_gather x1, waiting for transfers between devices: 0.01 us -> 131 us  [on_device(): gathered = lax.all_gather(piece, 'pair', axis=0, tiled=True)]
    all_gather x1 -> x0, other arithmetic: 114 us -> none  [on_device(): piece_tiles = lax.all_gather(int_tiles, 'pair', axis=1, tiled=True)]
    pallas_call x0 -> x3, Pallas kernels: none -> 60.3 us  [the longest x1 30.1 us: product(): pl.pallas_call(product_kernel, grid=(groups + steps,), out_shape=jax.Shap...]
    gather x6 -> x0, local copies, waits for them, and re-layouts: 59.1 us -> none  [one_block(): chosen = jnp.take(amp_local, contract_idx, axis=0)]
    scatter x3 -> x0, local copies, waits for them, and re-layouts: 34.7 us -> none  [the longest x1 19.5 us: on_device(): jnp.zeros((cells, flat), jnp.bfloat16).at[targets].set(arrived, mode='drop')]
    all_to_all x5 -> x0, local copies, waits for them, and re-layouts: 28.4 us -> none  [the longest x2 27.1 us: on_device(): lax.all_to_all(outgoing, ('pair', 'ctr'), split_axis=0, concat_axis=0, ti...]
  transfers between devices with their start and end apart: 4 -> 3, of which waited for: 1 -> 2; matrix products, arithmetic and copies ran while one was open for 8% -> 0% of each run, Pallas kernels for 0% -> 11%
where the time goes in v1:
time: 276 us
  waiting for transfers between devices  175 us (63%)
  Pallas kernels  60.3 us (22%)
  between operations  13.5 us (5%)
  local copies, waits for them, and re-layouts  12.8 us (5%)
  starting transfers between devices  11.7 us (4%)
  other arithmetic  2.96 us (1%)
    all_gather x1, waiting for transfers between devices, on_device(): gathered = lax.all_gather(piece, 'pair', axis=0, tiled=True)  131 us
    reduce_scatter x1, waiting for transfers between devices, on_device(): lax.psum_scatter(partial_value, 'ctr', scatter_dimension=0, tiled=True)  44 us
    pallas_call x1, Pallas kernels, product(): pl.pallas_call(product_kernel, grid=(groups + steps,), out_shape=jax.Shap...  30.1 us
    pallas_call x1, Pallas kernels, place_integrals(): pl.pallas_call(integral_kernel, grid=(JT // 4,), out_shape=jax.ShapeDtype...  24.3 us
    all_to_all x1, starting transfers between devices, on_device(): lax.all_to_all(outgoing, ('pair', 'ctr'), split_axis=0, concat_axis=0, ti...  11.6 us
    unnamed x8, local copies, waits for them, and re-layouts  10.9 us
    pallas_call x1, Pallas kernels, pack(): pl.pallas_call(pack_kernel, grid=(steps + 1,), out_shape=jax.ShapeDtypeSt...  5.89 us
  transfers between devices with their start and end apart: 3, of which 2 were waited for; matrix products, arithmetic and copies ran while one was open for 0% of the time, Pallas kernels for 11%

profile of v1, /device:TPU:0, one launch (start us, length us, event | category | flops | bytes accessed | tf_op | source)
XLA Modules:
  0.0 276.0 jit_solution(696073787380132731)
XLA Ops:
  6.5 0.0 all-gather.2.cloned.1.call-start
  6.5 1.2 reshape_squeeze.3
  7.8 0.1 reshape.11
  7.9 0.7 fusion.8
  8.6 0.1 stack_tile.8
  8.7 0.7 convert_bitcast_fusion
  9.3 0.1 stack_tile.9
  9.4 0.1 stack_reshape.4
  9.5 0.1 copy.22
  9.6 0.8 fusion.1
  10.4 0.0 all-gather.2.cloned.1.call-update
  10.4 0.7 fusion.6
  11.2 0.1 copy.20
  11.4 0.1 convert_reduce_fusion
  11.5 0.0 copy-start.3
  11.5 2.3 copy-done.3
  13.8 5.9 %pack.1 = bf16[1024,4736]{1,0:T(8,128)(2,1)S(1)} custom-call(s32[1,256]{1,0:T(1,128)S(1)} %bitcast.12, bf16[256,128]{1,0:T(8,128)(2,1)S(1)} %pad.8.lab_ref, bf16[256,9216]{1,0:T(8,128)(2,1)S(1)} %copy-done.3, bf16[256,9216]{1,0:T(8,128)(2,1)S(1)} %copy-done.3), custom_call_target="tpu_custom_call" | custom-call | tf_op jit(solution)/shard_map/pack/pallas_call | solution.py:63
  19.7 0.0 copy-start
  19.7 3.7 %copy-done = bf16[1024,4736]{1,0:T(8,128)(2,1)} copy-done((bf16[1024,4736]{1,0:T(8,128)(2,1)}, bf16[1024,4736]{1,0:T(8,128)(2,1)S(1)}, u32[]{:S(2)}) %copy-start) | copy-done | bytes 9699352
  23.4 11.6 %all-to-all-start = ((bf16[128,8,4736]{2,1,0:T(8,128)(2,1)}), bf16[128,8,4736]{2,1,0:T(8,128)(2,1)}, u32[]{:S(2)}, u32[]{:S(2)}) async-start(bf16[128,8,4736]{2,1,0:T(8,128)(2,1)} %bitcast.11), calls=%async_computation | async-start | bytes 19398656 | tf_op jit(solution)/shard_map/all_to_all | solution.py:236
  35.0 0.0 reduce-scatter.2.cloned.1.call-start
  35.1 130.7 %all-gather.2.cloned.1.call-done.lab_ref.tiles_ref = bf16[1152,2432]{1,0:T(8,128)(2,1)} async-done(((bf16[72,2432]{1,0:T(8,128)(2,1)}), bf16[1152,2432]{1,0:T(8,128)(2,1)}) %all-gather.2.cloned.1.call-update) | async-done | bytes 5603344 | tf_op jit(solution)/shard_map/all_gather | solution.py:229
  165.8 0.0 copy-start.1
  165.8 2.6 copy-done.1
  168.4 24.3 %integrals.1.b_ref = bf16[2304,2304]{1,0:T(8,128)(2,1)} custom-call(bf16[1152,2432]{1,0:T(8,128)(2,1)S(1)} %copy-done.1, bf16[1152,2432]{1,0:T(8,128)(2,1)S(1)} %copy-done.1), custom_call_target="tpu_custom_call" | custom-call | tf_op jit(solution)/shard_map/integrals/pallas_call | solution.py:122
  192.7 0.0 all-to-all-done
  192.7 30.1 %product.1 = bf16[1152,2304]{1,0:T(8,128)(2,1)S(1)} custom-call(s32[1]{0:T(128)} %bitcast.odd_ref, bf16[1024,4736]{1,0:T(8,128)(2,1)} %bitcast.3.lab_ref.low_ref.high_ref, bf16[1024,4736]{1,0:T(8,128)(2,1)} %bitcast.3.lab_ref.low_ref.high_ref, bf16[1024,4736]{1,0:T(8,128)(2,1)} %bitcast.3.lab_ref.low_ref.high_ref, bf16[2304,2304]{1,0:T(8,128)(2,1)} %integrals.1.b_ref), custom_call_target="tpu_custom_call" | custom-call | tf_op jit(solution)/shard_map/product/pallas_call | solution.py:194
  222.9 0.0 copy-start.2
  222.9 2.3 copy-done.2
  225.2 0.0 reduce-scatter.2.cloned.1.call-update
  225.2 44.0 %reduce-scatter.2.cloned.1.call-done = bf16[144,2304]{1,0:T(8,128)(2,1)} async-done(((bf16[1152,2304]{1,0:T(8,128)(2,1)}), bf16[144,2304]{1,0:T(8,128)(2,1)}) %reduce-scatter.2.cloned.1.call-update) | async-done | bytes 663568 | tf_op jit(solution)/shard_map/reduce_scatter | solution.py:240
  (10 shorter events, 0.1 us)
Async XLA Ops:
  6.5 159.3 %all-gather.2.cloned.1.call-start = ((), (), s32[]{:S(2)}) async-start(), calls=%async_computation.2 | async-start | bytes 5953536 | tf_op jit(solution)/shard_map/all_gather | solution.py:229
  11.5 2.3 copy-start.3
  19.7 3.7 %copy-start = (bf16[1024,4736]{1,0:T(8,128)(2,1)}, bf16[1024,4736]{1,0:T(8,128)(2,1)S(1)}, u32[]{:S(2)}) copy-start(bf16[1024,4736]{1,0:T(8,128)(2,1)S(1)} %pack.1) | copy-start | bytes 29097988
  23.4 169.3 %all-to-all-start = ((bf16[128,8,4736]{2,1,0:T(8,128)(2,1)}), bf16[128,8,4736]{2,1,0:T(8,128)(2,1)}, u32[]{:S(2)}, u32[]{:S(2)}) async-start(bf16[128,8,4736]{2,1,0:T(8,128)(2,1)} %bitcast.11), calls=%async_computation | async-start | bytes 19398656 | tf_op jit(solution)/shard_map/all_to_all | solution.py:236
  35.0 234.2 %reduce-scatter.2.cloned.1.call-start = ((), (), s32[]{:S(2)}) async-start(), calls=%async_computation.3 | async-start | bytes 5971968 | tf_op jit(solution)/shard_map/reduce_scatter | solution.py:240
  165.8 2.6 copy-start.1
  222.9 2.3 copy-start.2
Sparse Core Ops, SparseCore 0:
  10.5 155.2 all-gather.1
  225.3 43.8 reduce-scatter.1

commit v2 on v1

v2 whole, which is shorter than its diff:
```python
import jax
import jax.numpy as jnp
from jax import lax
from jax.experimental import pallas as pl
from jax.experimental.pallas import tpu as pltpu
from jax.sharding import PartitionSpec as P

TILE = 96
VT = 12
KT = 24
JT = 24
FLAT = TILE * TILE
HALF = FLAT // 2
QUARTER = FLAT // 4
SLOTS = 4
LANES = 128
MIB = 2**20


def quad_unpack(v0, v1, v2, lane):
    return (v0, jnp.where(lane >= 96, v0, v1), jnp.where(lane >= 64, v1, v2), v2)


def turn(x, amount):
    amount = amount % LANES
    return x if amount == 0 else pltpu.roll(x, amount, 1)


def pack_kernel(land_ref, lab_ref, low_ref, high_ref, out_ref, first, second):
    step = pl.program_id(0)
    rows = first.shape[0]

    @pl.when(step == 0)
    def _():
        row = lax.broadcasted_iota(jnp.int32, first.shape, 0)
        land = jnp.broadcast_to(land_ref[...], first.shape)
        first[...] = jnp.where(row == land, 1.0, 0.0).astype(jnp.bfloat16)
        second[...] = jnp.where((row ^ SLOTS) == land, 1.0, 0.0).astype(jnp.bfloat16)

    def spread(low, high):
        a = jnp.dot(first[...], low, preferred_element_type=jnp.float32)
        b = jnp.dot(second[...], high, preferred_element_type=jnp.float32)
        n = a.shape[1]
        a = a.reshape(rows // 8, 1, 8, n)
        b = b.reshape(rows // 8, 1, 8, n)
        top = lax.broadcasted_iota(jnp.int32, a.shape, 2) < SLOTS
        both = jnp.concatenate([jnp.where(top, a, b), jnp.where(top, b, a)], axis=1)
        return both.reshape(rows * 2, n).astype(jnp.bfloat16)

    @pl.when(step < pl.num_programs(0) - 1)
    def _():
        out_ref[...] = spread(low_ref[...], high_ref[...])

    @pl.when(step == pl.num_programs(0) - 1)
    def _():
        out_ref[:, :LANES] = spread(lab_ref[...], lab_ref[...])


def pack(land, labels, tiles, devices):
    held = tiles.shape[0]
    block = 512
    steps = HALF // block
    return pl.pallas_call(
        pack_kernel,
        grid=(steps + 1,),
        out_shape=jax.ShapeDtypeStruct((devices * 2 * SLOTS, HALF + LANES), jnp.bfloat16),
        in_specs=[
            pl.BlockSpec((1, held), lambda s: (0, 0)),
            pl.BlockSpec((held, LANES), lambda s: (0, 0)),
            pl.BlockSpec((held, block), lambda s: (0, jnp.minimum(s, steps - 1))),
            pl.BlockSpec((held, block), lambda s: (0, steps + jnp.minimum(s, steps - 1))),
        ],
        out_specs=pl.BlockSpec((devices * 2 * SLOTS, block), lambda s: (0, s)),
        scratch_shapes=[pltpu.VMEM((devices * SLOTS, held), jnp.bfloat16)] * 2,
        compiler_params=pltpu.CompilerParams(vmem_limit_bytes=56 * MIB),
        name="pack",
    )(land, labels, tiles, tiles)


def label_rows(lab):
    unit = (
        lax.broadcasted_iota(jnp.int32, (8, LANES), 0)
        == lax.broadcasted_iota(jnp.int32, (8, LANES), 1)
    )
    return lax.dot_general(
        jnp.where(unit, 1.0, 0.0).astype(jnp.bfloat16),
        lab,
        (((1,), (1,)), ((), ())),
        preferred_element_type=jnp.float32,
    )


def integral_kernel(k_ref, j_ref, tiles_ref, out_ref, spread):
    step = pl.program_id(0)
    held = (tiles_ref.shape[1] - 1) // TILE

    @pl.when(step == 0)
    def _():
        def clear(at, carry):
            spread[at] = jnp.zeros(spread.shape[1:], spread.dtype)
            return carry

        lax.fori_loop(0, JT, clear, 0)
        lane = lax.broadcasted_iota(jnp.int32, (TILE, LANES), 1)

        def source(at, carry):
            rows = pl.ds(pl.multiple_of(at * TILE, TILE), TILE)
            for quad in range(-(-held // 4)):
                v = [
                    tiles_ref[rows, (quad * 3 + n) * LANES : (quad * 3 + n + 1) * LANES].astype(jnp.float32)
                    if (quad * 3 + n) * LANES < tiles_ref.shape[1]
                    else None
                    for n in range(3)
                ]
                v = [v[0] if x is None else x for x in v]
                pieces = quad_unpack(*v, lane)
                for a in range(min(4, held - quad * 4)):
                    k = k_ref[at * held + quad * 4 + a]
                    j = j_ref[at * held + quad * 4 + a]
                    amount = (32 * a + 96 * (j % 4)) % LANES
                    spread[j, pl.ds(pl.multiple_of(k * TILE, TILE), TILE), :] = pltpu.roll(
                        pieces[a], amount, 1
                    ).astype(jnp.bfloat16)
            return carry

        lax.fori_loop(0, tiles_ref.shape[0] // TILE, source, 0)

    size = 256

    def join(at, carry):
        rows = pl.ds(pl.multiple_of(at * size, size), size)
        lane = lax.broadcasted_iota(jnp.int32, (size, LANES), 1)
        w = [spread[step * 4 + b, rows, :].astype(jnp.float32) for b in range(4)]
        out_ref[rows, 0:128] = jnp.where(lane < 96, w[0], w[1]).astype(jnp.bfloat16)
        out_ref[rows, 128:256] = jnp.where(lane < 64, w[1], w[2]).astype(jnp.bfloat16)
        out_ref[rows, 256:384] = jnp.where(lane < 32, w[2], w[3]).astype(jnp.bfloat16)
        return carry

    lax.fori_loop(0, KT * TILE // size, join, 0)


def place_integrals(k, j, gathered):
    return pl.pallas_call(
        integral_kernel,
        grid=(JT // 4,),
        out_shape=jax.ShapeDtypeStruct((KT * TILE, JT * TILE), jnp.bfloat16),
        in_specs=[
            pl.BlockSpec(memory_space=pltpu.SMEM),
            pl.BlockSpec(memory_space=pltpu.SMEM),
            pl.BlockSpec(gathered.shape, lambda s: (0, 0)),
        ],
        out_specs=pl.BlockSpec((KT * TILE, 4 * TILE), lambda s: (0, s)),
        scratch_shapes=[pltpu.VMEM((JT, KT * TILE, LANES), jnp.bfloat16)],
        compiler_params=pltpu.CompilerParams(vmem_limit_bytes=40 * MIB),
        name="integrals",
    )(k, j, gathered)


def product_kernel(odd_ref, from_ref, lab_ref, tiles_ref, b_ref, other_ref, own_ref, choose, amp, total):
    step = pl.program_id(0)
    groups = QUARTER // tiles_ref.shape[1]

    @pl.when(step == 0)
    def _():
        labels = label_rows(lab_ref[...])
        column = lax.broadcasted_iota(jnp.int32, (1, lab_ref.shape[0]), 1)
        second = ((column & SLOTS) // SLOTS) ^ odd_ref[0]
        k = labels[0:1].astype(jnp.int32) - 1
        i = labels[1:2].astype(jnp.int32)
        cell = k * (2 * VT) + second * VT + i
        row = lax.broadcasted_iota(jnp.int32, choose.shape, 0)
        choose[...] = jnp.where(row == jnp.broadcast_to(cell, choose.shape), 1.0, 0.0).astype(
            jnp.bfloat16
        )

    @pl.when(step < groups)
    def _():
        lane = lax.broadcasted_iota(jnp.int32, (48, LANES), 1)
        lane24 = lax.broadcasted_iota(jnp.int32, (24, LANES), 1)
        count = tiles_ref.shape[1] // 384
        for group in range(count):
            value = jnp.dot(
                choose[...],
                tiles_ref[:, group * 384 : (group + 1) * 384],
                preferred_element_type=jnp.float32,
            )
            for quad in range(KT // 4):
                pieces = []
                for b in range(4):
                    rows = value[(quad * 4 + b) * 24 : (quad * 4 + b + 1) * 24]
                    pieces.append(quad_unpack(rows[:, :128], rows[:, 128:256], rows[:, 256:], lane24))
                base = quad * 384
                for a in (0, 2):
                    w = [
                        jnp.concatenate([turn(pieces[b][a + c], 32 * (a + c - b)) for c in range(2)], axis=0)
                        for b in range(4)
                    ]
                    at = pl.ds(pl.multiple_of(((step * count + group) * 4 + a) * 24, 48), 48)
                    amp[at, base : base + 128] = jnp.where(lane < 96, w[0], w[1]).astype(jnp.bfloat16)
                    amp[at, base + 128 : base + 256] = jnp.where(lane < 64, w[1], w[2]).astype(jnp.bfloat16)
                    amp[at, base + 256 : base + 384] = jnp.where(lane < 32, w[2], w[3]).astype(jnp.bfloat16)

    @pl.when(step >= groups)
    def _():
        size = total.shape[0] * LANES
        for first in range(0, b_ref.shape[1], 256):
            value = jnp.dot(amp[...], b_ref[:, first : first + 256], preferred_element_type=jnp.float32)
            for part in range(2):
                lanes = slice(first + part * LANES, first + (part + 1) * LANES)
                slot = first // LANES + part
                total[slot] = value[:, part * LANES : (part + 1) * LANES]
                for n, ref in ((0, other_ref), (VT, own_ref)):
                    for pair in range(VT // 2):
                        rows = [
                            total[slot, pl.ds(from_ref[n + 2 * pair + q], 24, stride=24), :]
                            for q in range(2)
                        ]
                        ref[pair * 48 : (pair + 1) * 48, lanes] = jnp.concatenate(rows, axis=0).astype(
                            jnp.bfloat16
                        )


def product(odd, rows_from, labelled, label_at, arrived, lanes_at, integrals):
    wide = 768
    groups = QUARTER // wide
    block = 768
    steps = integrals.shape[1] // block
    rows = arrived.shape[0]
    half = VT * TILE // 4
    return pl.pallas_call(
        product_kernel,
        grid=(groups + steps,),
        out_shape=[jax.ShapeDtypeStruct((half, JT * TILE), jnp.bfloat16)] * 2,
        in_specs=[
            pl.BlockSpec(memory_space=pltpu.SMEM),
            pl.BlockSpec(memory_space=pltpu.SMEM),
            pl.BlockSpec((rows, LANES), lambda s: (0, label_at // LANES)),
            pl.BlockSpec((rows, wide), lambda s: (0, lanes_at // wide + jnp.minimum(s, groups - 1))),
            pl.BlockSpec((KT * TILE, block), lambda s: (0, jnp.maximum(s - groups, 0))),
        ],
        out_specs=[pl.BlockSpec((half, block), lambda s: (0, jnp.maximum(s - groups, 0)))] * 2,
        scratch_shapes=[
            pltpu.VMEM((2 * VT * KT, rows), jnp.bfloat16),
            pltpu.VMEM((VT * TILE // 2, KT * TILE), jnp.bfloat16),
            pltpu.VMEM((block // LANES, VT * TILE // 2, LANES), jnp.float32),
        ],
        compiler_params=pltpu.CompilerParams(vmem_limit_bytes=48 * MIB),
        name="product",
    )(odd, rows_from, labelled, arrived, integrals)


def exchange(other, own, ctr_count):
    depth = ctr_count // 2
    swap = [(c, c ^ 1) for c in range(ctr_count)]
    came = lax.ppermute(other, "ctr", swap)
    both = (own.astype(jnp.float32) + came.astype(jnp.float32)).astype(jnp.bfloat16)
    both = both.reshape(depth, -1, own.shape[1])
    total = both[0].astype(jnp.float32)
    parts = []
    for far in (2, 1, 3):
        move = [(c, (c // 2 + far) % depth * 2 + c % 2) for c in range(ctr_count)]
        parts.append(lax.ppermute(both[far], "ctr", move))
    for part in parts:
        total = total + part.astype(jnp.float32)
    return total.astype(jnp.bfloat16)


def lanes_of(columns):
    stacked = jnp.stack(columns, axis=1).astype(jnp.bfloat16)
    return jnp.pad(stacked, ((0, 0), (0, LANES - stacked.shape[1])))


def on_device(amp_tiles, amp_rows, amp_cols, int_tiles, int_rows, int_cols):
    ctr_count = lax.axis_size("ctr")
    devices = lax.axis_size("pair") * ctr_count
    held = amp_tiles.shape[0]
    count = int_rows.shape[1]
    square = int_tiles[0].reshape(count, TILE, TILE).transpose(1, 0, 2).reshape(TILE, count * TILE)
    spare = -(-(count * TILE) // LANES) * LANES - count * TILE
    int_labels = jnp.pad(
        jnp.concatenate([int_rows % KT, int_cols], axis=0).astype(jnp.bfloat16),
        ((0, TILE - 2), (0, spare - count)),
    )
    piece = jnp.concatenate([square, int_labels], axis=1)
    gathered = lax.all_gather(piece, "pair", axis=0, tiled=True)
    names = gathered.reshape(-1, TILE, piece.shape[1])[:, :2, count * TILE : count * TILE + count].astype(jnp.int32)
    target = amp_rows // VT * ctr_count + amp_cols // KT
    order = jnp.arange(held, dtype=jnp.int32)
    earlier = (target[:, None] == target[None, :]) & (order[:, None] < order[None, :])
    land = target * SLOTS + jnp.sum(earlier.astype(jnp.int32), axis=0)
    labels = lanes_of([amp_cols % KT + 1, amp_rows % VT])
    outgoing = pack(land[None, :], labels, amp_tiles, devices)
    arrived = lax.all_to_all(outgoing, ("pair", "ctr"), split_axis=0, concat_axis=0, tiled=True)
    integrals = place_integrals(names[:, 0].reshape(-1), names[:, 1].reshape(-1), gathered)
    ctr = lax.axis_index("ctr").astype(jnp.int32)
    odd, depth = ctr % 2, ctr // 2
    which = jnp.arange(2 * VT, dtype=jnp.int32)
    core = jnp.where(which < VT, 1 - odd, odd)
    owner = (depth + which % VT // 3) % (ctr_count // 2) * 2 + core
    block = 3 * owner + which % 3
    rows_from = block % 2 * VT + block // 2
    halves = []
    for half in range(2):
        other, own = product(odd.reshape(1), rows_from, arrived, HALF, arrived, half * QUARTER, integrals)
        halves.append(exchange(other, own, ctr_count).reshape(3, 24, -1))
    return jnp.stack(halves, axis=1).reshape(144, -1)


def solution(mesh):
    placed = (
        P(("pair", "ctr"), None),
        P(("pair", "ctr")),
        P(("pair", "ctr")),
        P("ctr", "pair", None),
        P("ctr", "pair"),
        P("ctr", "pair"),
    )
    return jax.shard_map(
        on_device, mesh=mesh, in_specs=placed, out_specs=P(("pair", "ctr"), None), check_vma=False
    )
```

time: 276 us -> 258 us (0.935)
  waiting for transfers between devices: 175 us -> 154 us
  starting transfers between devices: 11.7 us -> 22.3 us
  local copies, waits for them, and re-layouts: 12.8 us -> 6.56 us
  Pallas kernels: 60.3 us -> 55.2 us
    reduce_scatter x1 -> x0, waiting for transfers between devices: 44 us -> none  [on_device(): lax.psum_scatter(partial_value, 'ctr', scatter_dimension=0, tiled=True)]
    ppermute x0 -> x8, waiting for transfers between devices: none -> 23.1 us  [the longest x6 23.1 us: exchange(): parts.append(lax.ppermute(both[far], 'ctr', move))]
    pallas_call x1, Pallas kernels: 24.3 us -> 11.9 us  [place_integrals(): pl.pallas_call(integral_kernel, grid=(JT // 4,), out_shape=jax.ShapeDtype...]
    ppermute x0 -> x8, starting transfers between devices: none -> 10.7 us  [the longest x6 10.1 us: exchange(): parts.append(lax.ppermute(both[far], 'ctr', move))]
    unnamed x8 -> x10, local copies, waits for them, and re-layouts: 10.9 us -> 2.58 us
    pallas_call x1, Pallas kernels: 5.89 us -> 10.4 us  [pack(): pl.pallas_call(pack_kernel, grid=(steps + 1,), out_shape=jax.ShapeDtypeSt...]
    pallas_call x1 -> x2, Pallas kernels: 30.1 us -> 33 us  [product(): pl.pallas_call(product_kernel, grid=(groups + steps,), out_shape=[jax.Sha...]
  transfers between devices with their start and end apart: 3 -> 10, of which waited for: 2 -> 5; matrix products, arithmetic and copies ran while one was open for 0% -> 1% of each run, Pallas kernels for 11% -> 15%
where the time goes in v2:
time: 258 us; the launch traced here: 256 us
  waiting for transfers between devices  154 us (60%)
  Pallas kernels  55.2 us (21%)
  starting transfers between devices  22.3 us (9%)
  between operations  13.6 us (5%)
  local copies, waits for them, and re-layouts  6.56 us (3%)
  other arithmetic  3.58 us (1%)
    all_gather x1, waiting for transfers between devices, on_device(): gathered = lax.all_gather(piece, 'pair', axis=0, tiled=True)  131 us
    pallas_call x2, Pallas kernels, product(): pl.pallas_call(product_kernel, grid=(groups + steps,), out_shape=[jax.Sha...  33 us
    ppermute x6, waiting for transfers between devices, exchange(): parts.append(lax.ppermute(both[far], 'ctr', move))  23.1 us
    pallas_call x1, Pallas kernels, place_integrals(): pl.pallas_call(integral_kernel, grid=(JT // 4,), out_shape=jax.ShapeDtype...  11.9 us
    all_to_all x1, starting transfers between devices, on_device(): lax.all_to_all(outgoing, ('pair', 'ctr'), split_axis=0, concat_axis=0, ti...  11.6 us
    pallas_call x1, Pallas kernels, pack(): pl.pallas_call(pack_kernel, grid=(steps + 1,), out_shape=jax.ShapeDtypeSt...  10.4 us
    ppermute x6, starting transfers between devices, exchange(): parts.append(lax.ppermute(both[far], 'ctr', move))  10.1 us
  transfers between devices with their start and end apart: 10, of which 5 were waited for; matrix products, arithmetic and copies ran while one was open for 1% of the time, Pallas kernels for 15%

profile of v2, /device:TPU:0, one launch (start us, length us, event | category | flops | bytes accessed | tf_op | source)
XLA Modules:
  0.0 255.7 jit_solution(16327745815671167834)
XLA Ops:
  6.5 1.5 reshape_squeeze.9
  8.1 0.3 copy.19
  8.3 0.2 copy.20
  8.6 0.8 pad_maximum_fusion.1
  9.5 0.1 copy.18
  9.7 0.6 pad.8.lab_ref
  10.3 0.1 convert_reduce_fusion
  10.4 0.6 multiply_add_fusion
  11.0 10.4 %pack.1 = bf16[1024,4736]{1,0:T(8,128)(2,1)} custom-call(s32[1,256]{1,0:T(1,128)} %bitcast.16, bf16[256,128]{1,0:T(8,128)(2,1)} %pad.8.lab_ref, bf16[256,9216]{1,0:T(8,128)(2,1)} %high_ref.1, bf16[256,9216]{1,0:T(8,128)(2,1)} %high_ref.1), custom_call_target="tpu_custom_call" | custom-call | tf_op jit(solution)/shard_map/pack/pallas_call | solution.py:63
  21.4 11.6 %all-to-all-start = ((bf16[128,8,4736]{2,1,0:T(8,128)(2,1)}), bf16[128,8,4736]{2,1,0:T(8,128)(2,1)}, u32[]{:S(2)}, u32[]{:S(2)}) async-start(bf16[128,8,4736]{2,1,0:T(8,128)(2,1)} %bitcast.12), calls=%async_computation | async-start | bytes 19398656 | tf_op jit(solution)/shard_map/all_to_all | solution.py:293
  33.0 131.3 %all-gather.2.cloned.1.call-done.tiles_ref = bf16[1536,1792]{1,0:T(8,128)(2,1)} async-done(((bf16[96,1792]{1,0:T(8,128)(2,1)}), bf16[1536,1792]{1,0:T(8,128)(2,1)}) %all-gather.2.cloned.1.call-update) | async-done | bytes 5505040 | tf_op jit(solution)/shard_map/all_gather | solution.py:285
  164.4 0.8 slice_convert_fusion
  165.4 0.1 reshape_squeeze.11.j_ref
  165.5 2.6 copy-done
  168.0 11.9 %integrals.1.b_ref = bf16[2304,2304]{1,0:T(8,128)(2,1)} custom-call(s32[288]{0:T(512)S(1)} %reshape_squeeze.10.k_ref, s32[288]{0:T(512)S(1)} %reshape_squeeze.11.j_ref, bf16[1536,1792]{1,0:T(8,128)(2,1)S(1)} %copy-done), custom_call_target="tpu_custom_call" | custom-call | tf_op jit(solution)/shard_map/integrals/pallas_call | solution.py:143
  179.9 16.5 %product.2 = (bf16[288,2304]{1,0:T(8,128)(2,1)S(1)}, bf16[288,2304]{1,0:T(8,128)(2,1)S(1)}) custom-call(s32[1]{0:T(128)} %bitcast.odd_ref, s32[24]{0:T(128)S(1)} %fusion.15.from_ref, bf16[1024,4736]{1,0:T(8,128)(2,1)} %bitcast.3.lab_ref.tiles_ref, bf16[1024,4736]{1,0:T(8,128)(2,1)} %bitcast.3.lab_ref.tiles_ref, bf16[2304,2304]{1,0:T(8,128)(2,1)} %integrals.1.b_ref), custom_call_target="tpu_custom_call" | custom-call | tf_op jit(solution)/shard_map/product/pallas_call | solution.py:230
  196.4 0.1 collective-permute-start
  196.5 16.5 %product.3 = (bf16[288,2304]{1,0:T(8,128)(2,1)S(1)}, bf16[288,2304]{1,0:T(8,128)(2,1)S(1)}) custom-call(s32[1]{0:T(128)} %bitcast.odd_ref, s32[24]{0:T(128)S(1)} %fusion.15.from_ref, bf16[1024,4736]{1,0:T(8,128)(2,1)} %bitcast.3.lab_ref.tiles_ref, bf16[1024,4736]{1,0:T(8,128)(2,1)} %bitcast.3.lab_ref.tiles_ref, bf16[2304,2304]{1,0:T(8,128)(2,1)} %integrals.1.b_ref), custom_call_target="tpu_custom_call" | custom-call | tf_op jit(solution)/shard_map/product/pallas_call | solution.py:230
  213.0 0.5 collective-permute-start.4
  213.6 0.4 add_convert_fusion.1
  214.0 4.4 %collective-permute-start.1 = (bf16[72,2304]{1,0:T(8,128)(2,1)S(1)}, bf16[72,2304]{1,0:T(8,128)(2,1)S(1)}, u32[]{:S(2)}, u32[]{:S(2)}) collective-permute-start(bf16[72,2304]{1,0:T(8,128)(2,1)S(1)} %get-tuple-element.15), channel_id=1, source_target_pairs={{0,4},{1,5},{2,6},{3,7},{4,0},{5,1},{6,2},{7,3},{8,12},{9,13},{10,... | collective-permute-start | bytes 995336 | tf_op jit(solution)/shard_map/ppermute | solution.py:262
  218.4 3.2 %collective-permute-start.3 = (bf16[72,2304]{1,0:T(8,128)(2,1)S(1)}, bf16[72,2304]{1,0:T(8,128)(2,1)S(1)}, u32[]{:S(2)}, u32[]{:S(2)}) collective-permute-start(bf16[72,2304]{1,0:T(8,128)(2,1)S(1)} %get-tuple-element.16), channel_id=1, source_target_pairs={{0,6},{1,7},{2,0},{3,1},{4,2},{5,3},{6,4},{7,5},{8,14},{9,15},{10,... | collective-permute-start | bytes 995336 | tf_op jit(solution)/shard_map/ppermute | solution.py:262
  221.6 0.3 add_convert_fusion
  222.2 0.8 collective-permute-start.6
  223.0 4.0 %collective-permute-done.1 = bf16[72,2304]{1,0:T(8,128)(2,1)S(1)} collective-permute-done((bf16[72,2304]{1,0:T(8,128)(2,1)S(1)}, bf16[72,2304]{1,0:T(8,128)(2,1)S(1)}, u32[]{:S(2)}, u32[]{:S(2)}) %collective-permute-start.1) | collective-permute-done | bytes 331808 | tf_op jit(solution)/shard_map/ppermute | solution.py:262
  227.0 1.5 collective-permute-start.7
  228.5 5.7 %collective-permute-done.2 = bf16[72,2304]{1,0:T(8,128)(2,1)S(1)} collective-permute-done((bf16[72,2304]{1,0:T(8,128)(2,1)S(1)}, bf16[72,2304]{1,0:T(8,128)(2,1)S(1)}, u32[]{:S(2)}, u32[]{:S(2)}) %collective-permute-start.2) | collective-permute-done | bytes 331808 | tf_op jit(solution)/shard_map/ppermute | solution.py:262
  234.2 0.2 add_convert_fusion.3
  234.4 6.9 %collective-permute-done.5 = bf16[72,2304]{1,0:T(8,128)(2,1)S(1)} collective-permute-done((bf16[72,2304]{1,0:T(8,128)(2,1)S(1)}, bf16[72,2304]{1,0:T(8,128)(2,1)S(1)}, u32[]{:S(2)}, u32[]{:S(2)}) %collective-permute-start.5) | collective-permute-done | bytes 331808 | tf_op jit(solution)/shard_map/ppermute | solution.py:262
  241.3 6.5 %collective-permute-done.6 = bf16[72,2304]{1,0:T(8,128)(2,1)S(1)} collective-permute-done((bf16[72,2304]{1,0:T(8,128)(2,1)S(1)}, bf16[72,2304]{1,0:T(8,128)(2,1)S(1)}, u32[]{:S(2)}, u32[]{:S(2)}) %collective-permute-start.6) | collective-permute-done | bytes 331808 | tf_op jit(solution)/shard_map/ppermute | solution.py:262
  247.8 0.2 add_convert_fusion.2
  248.0 0.9 copy.21
  (31 shorter events, 0.6 us)
Async XLA Ops:
  6.5 2.0 copy-start.3
  6.5 2.0 copy-start.4
  6.5 157.8 %all-gather.2.cloned.1.call-start = ((), (), s32[]{:S(2)}) async-start(), calls=%async_computation.1 | async-start | bytes 5849088 | tf_op jit(solution)/shard_map/all_gather | solution.py:285
  8.0 1.4 copy-start.1
  8.1 1.4 copy-start.2
  21.4 158.5 %all-to-all-start = ((bf16[128,8,4736]{2,1,0:T(8,128)(2,1)}), bf16[128,8,4736]{2,1,0:T(8,128)(2,1)}, u32[]{:S(2)}, u32[]{:S(2)}) async-start(bf16[128,8,4736]{2,1,0:T(8,128)(2,1)} %bitcast.12), calls=%async_computation | async-start | bytes 19398656 | tf_op jit(solution)/shard_map/all_to_all | solution.py:293
  165.5 2.6 %copy-start = (bf16[1536,1792]{1,0:T(8,128)(2,1)S(1)}, bf16[1536,1792]{1,0:T(8,128)(2,1)}, u32[]{:S(2)}) copy-start(bf16[1536,1792]{1,0:T(8,128)(2,1)} %all-gather.2.cloned.1.call-done.tiles_ref) | copy-start | bytes 16515076
  196.4 17.2 %collective-permute-start = (bf16[288,2304]{1,0:T(8,128)(2,1)S(1)}, bf16[288,2304]{1,0:T(8,128)(2,1)S(1)}, u32[]{:S(2)}, u32[]{:S(2)}) collective-permute-start(bf16[288,2304]{1,0:T(8,128)(2,1)S(1)} %get-tuple-element.10), channel_id=1, source_target_pairs={{0,1},{1,0},{2,3},{3,2},{4,5},{5,4},{6,7},{7,6},{8,9},{9,8},{10,11... | collective-permute-start | bytes 3981320 | tf_op jit(solution)/shard_map/ppermute | solution.py:255
  213.0 8.6 %collective-permute-start.4 = (bf16[288,2304]{1,0:T(8,128)(2,1)S(1)}, bf16[288,2304]{1,0:T(8,128)(2,1)S(1)}, u32[]{:S(2)}, u32[]{:S(2)}) collective-permute-start(bf16[288,2304]{1,0:T(8,128)(2,1)S(1)} %get-tuple-element.12), channel_id=1, source_target_pairs={{0,1},{1,0},{2,3},{3,2},{4,5},{5,4},{6,7},{7,6},{8,9},{9,8},{10,11... | collective-permute-start | bytes 3981320 | tf_op jit(solution)/shard_map/ppermute | solution.py:255
  214.0 13.0 %collective-permute-start.1 = (bf16[72,2304]{1,0:T(8,128)(2,1)S(1)}, bf16[72,2304]{1,0:T(8,128)(2,1)S(1)}, u32[]{:S(2)}, u32[]{:S(2)}) collective-permute-start(bf16[72,2304]{1,0:T(8,128)(2,1)S(1)} %get-tuple-element.15), channel_id=1, source_target_pairs={{0,4},{1,5},{2,6},{3,7},{4,0},{5,1},{6,2},{7,3},{8,12},{9,13},{10,... | collective-permute-start | bytes 995336 | tf_op jit(solution)/shard_map/ppermute | solution.py:262
  218.4 15.8 %collective-permute-start.2 = (bf16[72,2304]{1,0:T(8,128)(2,1)S(1)}, bf16[72,2304]{1,0:T(8,128)(2,1)S(1)}, u32[]{:S(2)}, u32[]{:S(2)}) collective-permute-start(bf16[72,2304]{1,0:T(8,128)(2,1)S(1)} %get-tuple-element.17), channel_id=1, source_target_pairs={{0,2},{1,3},{2,4},{3,5},{4,6},{5,7},{6,0},{7,1},{8,10},{9,11},{10,... | collective-permute-start | bytes 995336 | tf_op jit(solution)/shard_map/ppermute | solution.py:262
  218.4 15.8 %collective-permute-start.3 = (bf16[72,2304]{1,0:T(8,128)(2,1)S(1)}, bf16[72,2304]{1,0:T(8,128)(2,1)S(1)}, u32[]{:S(2)}, u32[]{:S(2)}) collective-permute-start(bf16[72,2304]{1,0:T(8,128)(2,1)S(1)} %get-tuple-element.16), channel_id=1, source_target_pairs={{0,6},{1,7},{2,0},{3,1},{4,2},{5,3},{6,4},{7,5},{8,14},{9,15},{10,... | collective-permute-start | bytes 995336 | tf_op jit(solution)/shard_map/ppermute | solution.py:262
  222.1 19.2 %collective-permute-start.5 = (bf16[72,2304]{1,0:T(8,128)(2,1)S(1)}, bf16[72,2304]{1,0:T(8,128)(2,1)S(1)}, u32[]{:S(2)}, u32[]{:S(2)}) collective-permute-start(bf16[72,2304]{1,0:T(8,128)(2,1)S(1)} %get-tuple-element.18), channel_id=1, source_target_pairs={{0,4},{1,5},{2,6},{3,7},{4,0},{5,1},{6,2},{7,3},{8,12},{9,13},{10,... | collective-permute-start | bytes 995336 | tf_op jit(solution)/shard_map/ppermute | solution.py:262
  222.2 25.6 %collective-permute-start.6 = (bf16[72,2304]{1,0:T(8,128)(2,1)S(1)}, bf16[72,2304]{1,0:T(8,128)(2,1)S(1)}, u32[]{:S(2)}, u32[]{:S(2)}) collective-permute-start(bf16[72,2304]{1,0:T(8,128)(2,1)S(1)} %get-tuple-element.20), channel_id=1, source_target_pairs={{0,2},{1,3},{2,4},{3,5},{4,6},{5,7},{6,0},{7,1},{8,10},{9,11},{10,... | collective-permute-start | bytes 995336 | tf_op jit(solution)/shard_map/ppermute | solution.py:262
  227.0 20.7 %collective-permute-start.7 = (bf16[72,2304]{1,0:T(8,128)(2,1)S(1)}, bf16[72,2304]{1,0:T(8,128)(2,1)S(1)}, u32[]{:S(2)}, u32[]{:S(2)}) collective-permute-start(bf16[72,2304]{1,0:T(8,128)(2,1)S(1)} %get-tuple-element.19), channel_id=1, source_target_pairs={{0,6},{1,7},{2,0},{3,1},{4,2},{5,3},{6,4},{7,5},{8,14},{9,15},{10,... | collective-permute-start | bytes 995336 | tf_op jit(solution)/shard_map/ppermute | solution.py:262
Sparse Core Ops, SparseCore 0:
  9.6 154.7 all-gather.1

commit v3 on v2

v3 whole, which is shorter than its diff:
```python
import functools

import jax
import jax.numpy as jnp
from jax import lax
from jax.experimental import pallas as pl
from jax.experimental.pallas import tpu as pltpu
from jax.sharding import PartitionSpec as P

TILE = 96
VT = 12
KT = 24
JT = 24
FLAT = TILE * TILE
HALF = FLAT // 2
QUARTER = FLAT // 4
SLOTS = 4
LANES = 128
MIB = 2**20
QUADS = (6, 6)


def quad_unpack(v0, v1, v2, lane):
    return (v0, jnp.where(lane >= 96, v0, v1), jnp.where(lane >= 64, v1, v2), v2)


def turn(x, amount):
    amount = amount % LANES
    return x if amount == 0 else pltpu.roll(x, amount, 1)


def pack_kernel(labelled, land_ref, lab_ref, low_ref, high_ref, out_ref, first, second):
    step = pl.program_id(0)
    rows = first.shape[0]

    @pl.when(step == 0)
    def _():
        row = lax.broadcasted_iota(jnp.int32, first.shape, 0)
        land = jnp.broadcast_to(land_ref[...], first.shape)
        first[...] = jnp.where(row == land, 1.0, 0.0).astype(jnp.bfloat16)
        second[...] = jnp.where((row ^ SLOTS) == land, 1.0, 0.0).astype(jnp.bfloat16)

    def spread(low, high):
        a = jnp.dot(first[...], low, preferred_element_type=jnp.float32)
        b = jnp.dot(second[...], high, preferred_element_type=jnp.float32)
        n = a.shape[1]
        a = a.reshape(rows // 8, 1, 8, n)
        b = b.reshape(rows // 8, 1, 8, n)
        top = lax.broadcasted_iota(jnp.int32, a.shape, 2) < SLOTS
        both = jnp.concatenate([jnp.where(top, a, b), jnp.where(top, b, a)], axis=1)
        return both.reshape(rows * 2, n).astype(jnp.bfloat16)

    if not labelled:
        out_ref[...] = spread(low_ref[...], high_ref[...])
        return

    @pl.when(step < pl.num_programs(0) - 1)
    def _():
        out_ref[...] = spread(low_ref[...], high_ref[...])

    @pl.when(step == pl.num_programs(0) - 1)
    def _():
        out_ref[:, :LANES] = spread(lab_ref[...], lab_ref[...])


def pack(land, labels, tiles, devices, first_quad, quads, labelled):
    held = tiles.shape[0]
    block = 768
    steps = quads * 384 // block
    at = first_quad * 384 // block
    return pl.pallas_call(
        functools.partial(pack_kernel, labelled),
        grid=(steps + int(labelled),),
        out_shape=jax.ShapeDtypeStruct(
            (devices * 2 * SLOTS, quads * 384 + LANES * int(labelled)), jnp.bfloat16
        ),
        in_specs=[
            pl.BlockSpec((1, held), lambda s: (0, 0)),
            pl.BlockSpec((held, LANES), lambda s: (0, 0)),
            pl.BlockSpec((held, block), lambda s: (0, at + jnp.minimum(s, steps - 1))),
            pl.BlockSpec((held, block), lambda s: (0, at + HALF // block + jnp.minimum(s, steps - 1))),
        ],
        out_specs=pl.BlockSpec((devices * 2 * SLOTS, block), lambda s: (0, s)),
        scratch_shapes=[pltpu.VMEM((devices * SLOTS, held), jnp.bfloat16)] * 2,
        compiler_params=pltpu.CompilerParams(vmem_limit_bytes=56 * MIB),
        name="pack",
    )(land, labels, tiles, tiles)


def label_rows(lab):
    unit = (
        lax.broadcasted_iota(jnp.int32, (8, LANES), 0)
        == lax.broadcasted_iota(jnp.int32, (8, LANES), 1)
    )
    return lax.dot_general(
        jnp.where(unit, 1.0, 0.0).astype(jnp.bfloat16),
        lab,
        (((1,), (1,)), ((), ())),
        preferred_element_type=jnp.float32,
    )


def integral_kernel(k_ref, j_ref, tiles_ref, out_ref, spread):
    step = pl.program_id(0)
    held = (tiles_ref.shape[1] - 1) // TILE

    @pl.when(step == 0)
    def _():
        def clear(at, carry):
            spread[at] = jnp.zeros(spread.shape[1:], spread.dtype)
            return carry

        lax.fori_loop(0, JT, clear, 0)
        lane = lax.broadcasted_iota(jnp.int32, (TILE, LANES), 1)

        def source(at, carry):
            rows = pl.ds(pl.multiple_of(at * TILE, TILE), TILE)
            for quad in range(-(-held // 4)):
                v = [
                    tiles_ref[rows, (quad * 3 + n) * LANES : (quad * 3 + n + 1) * LANES].astype(jnp.float32)
                    if (quad * 3 + n) * LANES < tiles_ref.shape[1]
                    else None
                    for n in range(3)
                ]
                v = [v[0] if x is None else x for x in v]
                pieces = quad_unpack(*v, lane)
                for a in range(min(4, held - quad * 4)):
                    k = k_ref[at * held + quad * 4 + a]
                    j = j_ref[at * held + quad * 4 + a]
                    amount = (32 * a + 96 * (j % 4)) % LANES
                    spread[j, pl.ds(pl.multiple_of(k * TILE, TILE), TILE), :] = pltpu.roll(
                        pieces[a], amount, 1
                    ).astype(jnp.bfloat16)
            return carry

        lax.fori_loop(0, tiles_ref.shape[0] // TILE, source, 0)

    size = 256

    def join(at, carry):
        rows = pl.ds(pl.multiple_of(at * size, size), size)
        lane = lax.broadcasted_iota(jnp.int32, (size, LANES), 1)
        w = [spread[step * 4 + b, rows, :].astype(jnp.float32) for b in range(4)]
        out_ref[rows, 0:128] = jnp.where(lane < 96, w[0], w[1]).astype(jnp.bfloat16)
        out_ref[rows, 128:256] = jnp.where(lane < 64, w[1], w[2]).astype(jnp.bfloat16)
        out_ref[rows, 256:384] = jnp.where(lane < 32, w[2], w[3]).astype(jnp.bfloat16)
        return carry

    lax.fori_loop(0, KT * TILE // size, join, 0)


def place_integrals(k, j, gathered):
    return pl.pallas_call(
        integral_kernel,
        grid=(JT // 4,),
        out_shape=jax.ShapeDtypeStruct((KT * TILE, JT * TILE), jnp.bfloat16),
        in_specs=[
            pl.BlockSpec(memory_space=pltpu.SMEM),
            pl.BlockSpec(memory_space=pltpu.SMEM),
            pl.BlockSpec(gathered.shape, lambda s: (0, 0)),
        ],
        out_specs=pl.BlockSpec((KT * TILE, 4 * TILE), lambda s: (0, s)),
        scratch_shapes=[pltpu.VMEM((JT, KT * TILE, LANES), jnp.bfloat16)],
        compiler_params=pltpu.CompilerParams(vmem_limit_bytes=40 * MIB),
        name="integrals",
    )(k, j, gathered)


def choose_kernel(odd_ref, lab_ref, choose_ref):
    labels = label_rows(lab_ref[...])
    column = lax.broadcasted_iota(jnp.int32, (1, lab_ref.shape[0]), 1)
    second = ((column & SLOTS) // SLOTS) ^ odd_ref[0]
    k = labels[0:1].astype(jnp.int32) - 1
    i = labels[1:2].astype(jnp.int32)
    cell = k * (2 * VT) + second * VT + i
    row = lax.broadcasted_iota(jnp.int32, choose_ref.shape, 0)
    choose_ref[...] = jnp.where(row == jnp.broadcast_to(cell, choose_ref.shape), 1.0, 0.0).astype(
        jnp.bfloat16
    )


def choosing(odd, labelled):
    rows = labelled.shape[0]
    return pl.pallas_call(
        choose_kernel,
        grid=(1,),
        out_shape=jax.ShapeDtypeStruct((2 * VT * KT, rows), jnp.bfloat16),
        in_specs=[
            pl.BlockSpec(memory_space=pltpu.SMEM),
            pl.BlockSpec((rows, LANES), lambda s: (0, labelled.shape[1] // LANES - 1)),
        ],
        out_specs=pl.BlockSpec((2 * VT * KT, rows), lambda s: (0, 0)),
        compiler_params=pltpu.CompilerParams(vmem_limit_bytes=58 * MIB),
        name="choose",
    )(odd, labelled)


def place_kernel(choose_ref, tiles_ref, out_ref):
    lane = lax.broadcasted_iota(jnp.int32, (48, LANES), 1)
    lane24 = lax.broadcasted_iota(jnp.int32, (24, LANES), 1)
    for group in range(2):
        value = jnp.dot(
            choose_ref[...],
            tiles_ref[:, group * 384 : (group + 1) * 384],
            preferred_element_type=jnp.float32,
        )
        for quad in range(KT // 4):
            pieces = []
            for b in range(4):
                rows = value[(quad * 4 + b) * 24 : (quad * 4 + b + 1) * 24]
                pieces.append(quad_unpack(rows[:, :128], rows[:, 128:256], rows[:, 256:], lane24))
            base = quad * 384
            for a in (0, 2):
                w = [
                    jnp.concatenate([turn(pieces[b][a + c], 32 * (a + c - b)) for c in range(2)], axis=0)
                    for b in range(4)
                ]
                at = slice((group * 4 + a) * 24, (group * 4 + a) * 24 + 48)
                out_ref[at, base : base + 128] = jnp.where(lane < 96, w[0], w[1]).astype(jnp.bfloat16)
                out_ref[at, base + 128 : base + 256] = jnp.where(lane < 64, w[1], w[2]).astype(jnp.bfloat16)
                out_ref[at, base + 256 : base + 384] = jnp.where(lane < 32, w[2], w[3]).astype(jnp.bfloat16)


def place(choose, arrived, quads):
    return pl.pallas_call(
        place_kernel,
        grid=(quads // 2,),
        out_shape=jax.ShapeDtypeStruct((quads * 96, KT * TILE), jnp.bfloat16),
        in_specs=[
            pl.BlockSpec(choose.shape, lambda s: (0, 0)),
            pl.BlockSpec((arrived.shape[0], 768), lambda s: (0, s)),
        ],
        out_specs=pl.BlockSpec((192, KT * TILE), lambda s: (s, 0)),
        compiler_params=pltpu.CompilerParams(vmem_limit_bytes=58 * MIB),
        name="place",
    )(choose, arrived)


def product_kernel(from_ref, amp_ref, b_ref, *refs):
    outs, total = refs[:-1], refs[-1]
    each = 2 * VT // len(outs)
    depth = amp_ref.shape[0] // (2 * VT)
    joined = 1 if depth % 16 == 0 else 2
    for first in range(0, b_ref.shape[1], 256):
        value = jnp.dot(amp_ref[...], b_ref[:, first : first + 256], preferred_element_type=jnp.float32)
        for part in range(2):
            lanes = slice(first + part * LANES, first + (part + 1) * LANES)
            slot = first // LANES + part
            total[slot] = value[:, part * LANES : (part + 1) * LANES]
            for n, ref in enumerate(outs):
                for at in range(0, each, joined):
                    rows = [
                        total[slot, pl.ds(from_ref[n * each + at + q], depth, stride=2 * VT), :]
                        for q in range(joined)
                    ]
                    ref[at * depth : (at + joined) * depth, lanes] = jnp.concatenate(rows, axis=0).astype(
                        jnp.bfloat16
                    )


def product(rows_from, amp, integrals, outputs):
    block = 768
    size = amp.shape[0] // outputs
    return pl.pallas_call(
        product_kernel,
        grid=(integrals.shape[1] // block,),
        out_shape=[jax.ShapeDtypeStruct((size, JT * TILE), jnp.bfloat16)] * outputs,
        in_specs=[
            pl.BlockSpec(memory_space=pltpu.SMEM),
            pl.BlockSpec(amp.shape, lambda s: (0, 0)),
            pl.BlockSpec((KT * TILE, block), lambda s: (0, s)),
        ],
        out_specs=[pl.BlockSpec((size, block), lambda s: (0, s))] * outputs,
        scratch_shapes=[pltpu.VMEM((block // LANES, amp.shape[0], LANES), jnp.float32)],
        compiler_params=pltpu.CompilerParams(vmem_limit_bytes=58 * MIB),
        name="product",
    )(rows_from, amp, integrals)


def swap_cores(other, own, ctr_count):
    swap = [(c, c ^ 1) for c in range(ctr_count)]
    came = lax.ppermute(other, "ctr", swap)
    return (own.astype(jnp.float32) + came.astype(jnp.float32)).astype(jnp.bfloat16)


def sum_depths(both, ctr_count):
    depth = ctr_count // 2
    both = both.reshape(depth, -1, both.shape[1])
    total = both[0].astype(jnp.float32)
    parts = []
    for far in (2, 1, 3):
        move = [(c, (c // 2 + far) % depth * 2 + c % 2) for c in range(ctr_count)]
        parts.append(lax.ppermute(both[far], "ctr", move))
    for part in parts:
        total = total + part.astype(jnp.float32)
    return total.astype(jnp.bfloat16)


def lanes_of(columns):
    stacked = jnp.stack(columns, axis=1).astype(jnp.bfloat16)
    return jnp.pad(stacked, ((0, 0), (0, LANES - stacked.shape[1])))


def on_device(amp_tiles, amp_rows, amp_cols, int_tiles, int_rows, int_cols):
    ctr_count = lax.axis_size("ctr")
    devices = lax.axis_size("pair") * ctr_count
    held = amp_tiles.shape[0]
    count = int_rows.shape[1]
    square = int_tiles[0].reshape(count, TILE, TILE).transpose(1, 0, 2).reshape(TILE, count * TILE)
    spare = -(-(count * TILE) // LANES) * LANES - count * TILE
    int_labels = jnp.pad(
        jnp.concatenate([int_rows % KT, int_cols], axis=0).astype(jnp.bfloat16),
        ((0, TILE - 2), (0, spare - count)),
    )
    piece = jnp.concatenate([square, int_labels], axis=1)
    gathered = lax.all_gather(piece, "pair", axis=0, tiled=True)
    target = amp_rows // VT * ctr_count + amp_cols // KT
    order = jnp.arange(held, dtype=jnp.int32)
    earlier = (target[:, None] == target[None, :]) & (order[:, None] < order[None, :])
    land = target * SLOTS + jnp.sum(earlier.astype(jnp.int32), axis=0)
    labels = lanes_of([amp_cols % KT + 1, amp_rows % VT])
    everyone = ("pair", "ctr")
    packed = [
        pack(land[None, :], labels, amp_tiles, devices, sum(QUADS[:n]), quads, n == 0)
        for n, quads in enumerate(QUADS)
    ]
    packed = lax.optimization_barrier(packed)
    arrived = [
        lax.all_to_all(outgoing, everyone, split_axis=0, concat_axis=0, tiled=True) for outgoing in packed
    ]
    ctr = lax.axis_index("ctr").astype(jnp.int32)
    odd, depth = ctr % 2, ctr // 2
    which = jnp.arange(2 * VT, dtype=jnp.int32)
    core = jnp.where(which < VT, 1 - odd, odd)
    owner = (depth + which % VT // 3) % (ctr_count // 2) * 2 + core
    block = 3 * owner + which % 3
    spread_rows = block % 2 * VT + block // 2
    block = jnp.arange(2 * VT, dtype=jnp.int32)
    natural_rows = block % 2 * VT + block // 2
    names = gathered.reshape(-1, TILE, piece.shape[1])[:, :2, count * TILE : count * TILE + count]
    names = names.astype(jnp.int32)
    integrals = place_integrals(names[:, 0].reshape(-1), names[:, 1].reshape(-1), gathered)
    arrived[0], integrals = lax.optimization_barrier((arrived[0], integrals))
    choose = choosing(odd.reshape(1), arrived[0])
    parts = []
    for n, quads in enumerate(QUADS):
        amp = place(choose, arrived[n], quads)
        if n < len(QUADS) - 1:
            [value] = product(natural_rows, amp, integrals, 1)
            parts.append(lax.psum_scatter(value, "ctr", scatter_dimension=0, tiled=True))
        else:
            both = swap_cores(*product(spread_rows, amp, integrals, 2), ctr_count)
            parts.append(sum_depths(both, ctr_count))
    parts = [part.reshape(3, quads * 4, -1) for part, quads in zip(parts, QUADS)]
    return jnp.concatenate(parts, axis=1).reshape(144, -1)


def solution(mesh):
    placed = (
        P(("pair", "ctr"), None),
        P(("pair", "ctr")),
        P(("pair", "ctr")),
        P("ctr", "pair", None),
        P("ctr", "pair"),
        P("ctr", "pair"),
    )
    return jax.shard_map(
        on_device, mesh=mesh, in_specs=placed, out_specs=P(("pair", "ctr"), None), check_vma=False
    )
```

time: 258 us -> 236 us (0.915)
  waiting for transfers between devices: 154 us -> 37.9 us
  blocking collectives: 0 us -> 94.8 us
  starting transfers between devices: 22.3 us -> 9.12 us
  Pallas kernels: 55.2 us -> 64.4 us
  other arithmetic: 3.58 us -> 8.54 us
    all_gather x1, waiting for transfers between devices: 131 us -> 0.01 us  [on_device(): gathered = lax.all_gather(piece, 'pair', axis=0, tiled=True)]
    all_to_all x0 -> x1, blocking collectives: none -> 94.8 us  [on_device(): lax.all_to_all(outgoing, everyone, split_axis=0, concat_axis=0, tiled=True)]
    all_to_all x1, waiting for transfers between devices: 0.01 us -> 19.3 us  [on_device(): lax.all_to_all(outgoing, everyone, split_axis=0, concat_axis=0, tiled=True)]
    pallas_call x3 -> x7, Pallas kernels: 43.3 us -> 52.6 us  [the longest x2 24.3 us: product(): pl.pallas_call(product_kernel, grid=(integrals.shape[1] // block,), out_s...]
    ppermute x8 -> x4, starting transfers between devices: 10.7 us -> 3.3 us  [the longest x3 3.29 us: sum_depths(): parts.append(lax.ppermute(both[far], 'ctr', move))]
    all_to_all x1, starting transfers between devices: 11.6 us -> 5.78 us  [on_device(): lax.all_to_all(outgoing, everyone, split_axis=0, concat_axis=0, tiled=True)]
    ppermute x8 -> x4, waiting for transfers between devices: 23.1 us -> 18.5 us  [the longest x3 15.2 us: sum_depths(): parts.append(lax.ppermute(both[far], 'ctr', move))]
  transfers between devices with their start and end apart: 10 -> 7, of which waited for: 5 -> 5; matrix products, arithmetic and copies ran while one was open for 1% -> 2% of each run, Pallas kernels for 15% -> 28%
where the time goes in v3:
time: 236 us; the launch traced here: 234 us
  blocking collectives  94.8 us (40%)
  Pallas kernels  64.4 us (27%)
  waiting for transfers between devices  37.9 us (16%)
  between operations  13.6 us (6%)
  starting transfers between devices  9.12 us (4%)
  other arithmetic  8.54 us (4%)
  local copies, waits for them, and re-layouts  5.58 us (2%)
    all_to_all x1, blocking collectives, on_device(): lax.all_to_all(outgoing, everyone, split_axis=0, concat_axis=0, tiled=True)  94.8 us
    pallas_call x2, Pallas kernels, product(): pl.pallas_call(product_kernel, grid=(integrals.shape[1] // block,), out_s...  24.3 us
    all_to_all x1, waiting for transfers between devices, on_device(): lax.all_to_all(outgoing, everyone, split_axis=0, concat_axis=0, tiled=True)  19.3 us
    ppermute x3, waiting for transfers between devices, sum_depths(): parts.append(lax.ppermute(both[far], 'ctr', move))  15.2 us
    pallas_call x2, Pallas kernels, place(): pl.pallas_call(place_kernel, grid=(quads // 2,), out_shape=jax.ShapeDtype...  14.8 us
    pallas_call x1, Pallas kernels, place_integrals(): pl.pallas_call(integral_kernel, grid=(JT // 4,), out_shape=jax.ShapeDtype...  11.8 us
    pallas_call x2, Pallas kernels, pack(): pl.pallas_call(functools.partial(pack_kernel, labelled), grid=(steps + in...  10.9 us
    all_to_all x1, starting transfers between devices, on_device(): lax.all_to_all(outgoing, everyone, split_axis=0, concat_axis=0, tiled=True)  5.78 us
  transfers between devices with their start and end apart: 7, of which 5 were waited for; matrix products, arithmetic and copies ran while one was open for 2% of the time, Pallas kernels for 28%

profile of v3, /device:TPU:0, one launch (start us, length us, event | category | flops | bytes accessed | tf_op | source)
XLA Modules:
  0.0 234.0 jit_solution(16719000166897635822)
XLA Ops:
  6.5 0.7 fusion.14
  7.2 0.7 convert.17
  7.9 1.5 reshape_squeeze.9
  9.4 0.3 copy.16
  9.6 0.2 copy.17
  9.9 0.8 pad_maximum_fusion.1
  10.9 0.6 pad.8.lab_ref
  11.7 0.5 multiply_add_fusion
  12.2 5.4 %pack.3 = bf16[1024,2304]{1,0:T(8,128)(2,1)} custom-call(s32[1,256]{1,0:T(1,128)} %bitcast.21, bf16[256,128]{1,0:T(8,128)(2,1)} %pad.8.lab_ref, bf16[256,9216]{1,0:T(8,128)(2,1)} %high_ref.3, bf16[256,9216]{1,0:T(8,128)(2,1)} %high_ref.3), custom_call_target="tpu_custom_call" | custom-call | tf_op jit(solution)/shard_map/pack/pallas_call | solution.py:71
  17.6 5.5 %pack.2 = bf16[1024,2432]{1,0:T(8,128)(2,1)} custom-call(s32[1,256]{1,0:T(1,128)} %bitcast.22, bf16[256,128]{1,0:T(8,128)(2,1)} %pad.8.lab_ref, bf16[256,9216]{1,0:T(8,128)(2,1)} %high_ref.3, bf16[256,9216]{1,0:T(8,128)(2,1)} %high_ref.3), custom_call_target="tpu_custom_call" | custom-call | tf_op jit(solution)/shard_map/pack/pallas_call | solution.py:71
  23.1 94.8 %all_to_all.23 = bf16[128,8,2432]{2,1,0:T(8,128)(2,1)} all-to-all(bf16[128,8,2432]{2,1,0:T(8,128)(2,1)} %bitcast.16), channel_id=1, replica_groups=mesh['pair'=16,'ctr'=8] {'pair','ctr'}, dimensions={0} | all-to-all | bytes 9961472 | tf_op jit(solution)/shard_map/all_to_all | solution.py:329
  117.9 5.8 %all-to-all-start.1 = ((bf16[128,8,2304]{2,1,0:T(8,128)(2,1)}), bf16[128,8,2304]{2,1,0:T(8,128)(2,1)}, u32[]{:S(2)}, u32[]{:S(2)}) async-start(bf16[128,8,2304]{2,1,0:T(8,128)(2,1)} %bitcast.17), calls=%async_computation.2 | async-start | bytes 9437184 | tf_op jit(solution)/shard_map/all_to_all | solution.py:329
  123.8 0.6 fusion.12.from_ref
  124.3 0.8 slice_convert_fusion
  125.4 2.6 %copy-done = bf16[1536,1792]{1,0:T(8,128)(2,1)S(1)} copy-done((bf16[1536,1792]{1,0:T(8,128)(2,1)S(1)}, bf16[1536,1792]{1,0:T(8,128)(2,1)}, u32[]{:S(2)}) %copy-start) | copy-done | bytes 5505048
  128.0 11.8 %integrals.1.b_ref = bf16[2304,2304]{1,0:T(8,128)(2,1)} custom-call(s32[288]{0:T(512)S(1)} %reshape_squeeze.10.k_ref, s32[288]{0:T(512)S(1)} %reshape_squeeze.11.j_ref, bf16[1536,1792]{1,0:T(8,128)(2,1)S(1)} %copy-done), custom_call_target="tpu_custom_call" | custom-call | tf_op jit(solution)/shard_map/integrals/pallas_call | solution.py:153
  139.8 2.7 %choose.1.choose_ref = bf16[576,1024]{1,0:T(8,128)(2,1)} custom-call(s32[1]{0:T(128)} %bitcast.odd_ref, bf16[1024,2432]{1,0:T(8,128)(2,1)} %bitcast.14), custom_call_target="tpu_custom_call" | custom-call | tf_op jit(solution)/shard_map/choose/pallas_call | solution.py:184
  142.5 7.4 %place.2.amp_ref = bf16[576,2304]{1,0:T(8,128)(2,1)} custom-call(bf16[576,1024]{1,0:T(8,128)(2,1)} %choose.1.choose_ref, bf16[1024,2432]{1,0:T(8,128)(2,1)} %bitcast.15), custom_call_target="tpu_custom_call" | custom-call | tf_op jit(solution)/shard_map/place/pallas_call | solution.py:225
  149.8 12.1 %product.2 = bf16[576,2304]{1,0:T(8,128)(2,1)} custom-call(s32[24]{0:T(128)} %fusion.12.from_ref, bf16[576,2304]{1,0:T(8,128)(2,1)} %place.2.amp_ref, bf16[2304,2304]{1,0:T(8,128)(2,1)} %integrals.1.b_ref), custom_call_target="tpu_custom_call" | custom-call | tf_op jit(solution)/shard_map/product/pallas_call | solution.py:264
  162.0 0.6 fusion.18.from_ref
  162.6 19.3 %all-to-all-done.1 = bf16[128,8,2304]{2,1,0:T(8,128)(2,1)} async-done(((bf16[128,8,2304]{2,1,0:T(8,128)(2,1)}), bf16[128,8,2304]{2,1,0:T(8,128)(2,1)}, u32[]{:S(2)}, u32[]{:S(2)}) %all-to-all-start.1) | async-done | bytes 4718624 | tf_op jit(solution)/shard_map/all_to_all | solution.py:329
  181.9 7.4 %place.3.amp_ref = bf16[576,2304]{1,0:T(8,128)(2,1)} custom-call(bf16[576,1024]{1,0:T(8,128)(2,1)} %choose.1.choose_ref, bf16[1024,2304]{1,0:T(8,128)(2,1)} %bitcast.9.tiles_ref), custom_call_target="tpu_custom_call" | custom-call | tf_op jit(solution)/shard_map/place/pallas_call | solution.py:225
  189.3 12.2 %product.3 = (bf16[288,2304]{1,0:T(8,128)(2,1)}, bf16[288,2304]{1,0:T(8,128)(2,1)}) custom-call(s32[24]{0:T(128)} %fusion.18.from_ref, bf16[576,2304]{1,0:T(8,128)(2,1)} %place.3.amp_ref, bf16[2304,2304]{1,0:T(8,128)(2,1)} %integrals.1.b_ref), custom_call_target="tpu_custom_call" | custom-call | tf_op jit(solution)/shard_map/product/pallas_call | solution.py:264
  201.5 3.3 %collective-permute-done = bf16[288,2304]{1,0:T(8,128)(2,1)S(1)} collective-permute-done((bf16[288,2304]{1,0:T(8,128)(2,1)}, bf16[288,2304]{1,0:T(8,128)(2,1)S(1)}, u32[]{:S(2)}, u32[]{:S(2)}) %collective-permute-start) | collective-permute-done | bytes 1327136 | tf_op jit(solution)/shard_map/ppermute | solution.py:282
  204.8 1.7 add_convert_fusion
  206.5 0.1 collective-permute-start.1
  206.7 3.1 %collective-permute-start.3 = (bf16[72,2304]{1,0:T(8,128)(2,1)S(1)}, bf16[72,2304]{1,0:T(8,128)(2,1)S(1)}, u32[]{:S(2)}, u32[]{:S(2)}) collective-permute-start(bf16[72,2304]{1,0:T(8,128)(2,1)S(1)} %get-tuple-element.20), channel_id=1, source_target_pairs={{0,6},{1,7},{2,0},{3,1},{4,2},{5,3},{6,4},{7,5},{8,14},{9,15},{10,... | collective-permute-start | bytes 995336 | tf_op jit(solution)/shard_map/ppermute | solution.py:293
  209.8 9.0 %collective-permute-done.1 = bf16[72,2304]{1,0:T(8,128)(2,1)S(1)} collective-permute-done((bf16[72,2304]{1,0:T(8,128)(2,1)S(1)}, bf16[72,2304]{1,0:T(8,128)(2,1)S(1)}, u32[]{:S(2)}, u32[]{:S(2)}) %collective-permute-start.1) | collective-permute-done | bytes 331808 | tf_op jit(solution)/shard_map/ppermute | solution.py:293
  218.8 3.8 %collective-permute-done.3 = bf16[72,2304]{1,0:T(8,128)(2,1)S(1)} collective-permute-done((bf16[72,2304]{1,0:T(8,128)(2,1)S(1)}, bf16[72,2304]{1,0:T(8,128)(2,1)S(1)}, u32[]{:S(2)}, u32[]{:S(2)}) %collective-permute-start.3) | collective-permute-done | bytes 331808 | tf_op jit(solution)/shard_map/ppermute | solution.py:293
  222.5 2.5 %collective-permute-done.2 = bf16[72,2304]{1,0:T(8,128)(2,1)S(1)} collective-permute-done((bf16[72,2304]{1,0:T(8,128)(2,1)S(1)}, bf16[72,2304]{1,0:T(8,128)(2,1)S(1)}, u32[]{:S(2)}, u32[]{:S(2)}) %collective-permute-start.2) | collective-permute-done | bytes 331808 | tf_op jit(solution)/shard_map/ppermute | solution.py:293
  225.0 0.2 add_convert_fusion.1
  225.3 1.9 pad_maximum_fusion
  (24 shorter events, 0.7 us)
Async XLA Ops:
  6.5 4.2 %copy-start.1 = (s32[256]{0:T(256)S(1)}, s32[256]{0:T(256)}, u32[]{:S(2)}) copy-start(s32[256]{0:T(256)} %param.8) | copy-start | bytes 3076
  6.5 4.2 %copy-start.2 = (s32[256]{0:T(256)S(1)}, s32[256]{0:T(256)}, u32[]{:S(2)}) copy-start(s32[256]{0:T(256)} %param.7) | copy-start | bytes 3076
  6.5 117.8 %all-gather.2.cloned.1.call-start = ((), (), s32[]{:S(2)}) async-start(), calls=%async_computation.3 | async-start | bytes 5849088 | tf_op jit(solution)/shard_map/all_gather | solution.py:316
  117.9 64.0 %all-to-all-start.1 = ((bf16[128,8,2304]{2,1,0:T(8,128)(2,1)}), bf16[128,8,2304]{2,1,0:T(8,128)(2,1)}, u32[]{:S(2)}, u32[]{:S(2)}) async-start(bf16[128,8,2304]{2,1,0:T(8,128)(2,1)} %bitcast.17), calls=%async_computation.2 | async-start | bytes 9437184 | tf_op jit(solution)/shard_map/all_to_all | solution.py:329
  123.7 101.5 %reduce-scatter.2.cloned.1.call-start = ((), (), s32[]{:S(2)}) async-start(), calls=%async_computation.4 | async-start | bytes 2985984 | tf_op jit(solution)/shard_map/reduce_scatter | solution.py:350
  125.4 2.6 %copy-start = (bf16[1536,1792]{1,0:T(8,128)(2,1)S(1)}, bf16[1536,1792]{1,0:T(8,128)(2,1)}, u32[]{:S(2)}) copy-start(bf16[1536,1792]{1,0:T(8,128)(2,1)} %all-gather.2.cloned.1.call-done.tiles_ref) | copy-start | bytes 16515076
  201.5 3.3 %collective-permute-start = (bf16[288,2304]{1,0:T(8,128)(2,1)}, bf16[288,2304]{1,0:T(8,128)(2,1)S(1)}, u32[]{:S(2)}, u32[]{:S(2)}) collective-permute-start(bf16[288,2304]{1,0:T(8,128)(2,1)} %get-tuple-element.16), channel_id=1, source_target_pairs={{0,1},{1,0},{2,3},{3,2},{4,5},{5,4},{6,7},{7,6},{8,9},{9,8},{10,11... | collective-permute-start | bytes 3981320 | tf_op jit(solution)/shard_map/ppermute | solution.py:282
  206.5 12.3 %collective-permute-start.1 = (bf16[72,2304]{1,0:T(8,128)(2,1)S(1)}, bf16[72,2304]{1,0:T(8,128)(2,1)S(1)}, u32[]{:S(2)}, u32[]{:S(2)}) collective-permute-start(bf16[72,2304]{1,0:T(8,128)(2,1)S(1)} %get-tuple-element.19), channel_id=1, source_target_pairs={{0,4},{1,5},{2,6},{3,7},{4,0},{5,1},{6,2},{7,3},{8,12},{9,13},{10,... | collective-permute-start | bytes 995336 | tf_op jit(solution)/shard_map/ppermute | solution.py:293
  206.7 15.9 %collective-permute-start.3 = (bf16[72,2304]{1,0:T(8,128)(2,1)S(1)}, bf16[72,2304]{1,0:T(8,128)(2,1)S(1)}, u32[]{:S(2)}, u32[]{:S(2)}) collective-permute-start(bf16[72,2304]{1,0:T(8,128)(2,1)S(1)} %get-tuple-element.20), channel_id=1, source_target_pairs={{0,6},{1,7},{2,0},{3,1},{4,2},{5,3},{6,4},{7,5},{8,14},{9,15},{10,... | collective-permute-start | bytes 995336 | tf_op jit(solution)/shard_map/ppermute | solution.py:293
  209.8 15.2 %collective-permute-start.2 = (bf16[72,2304]{1,0:T(8,128)(2,1)S(1)}, bf16[72,2304]{1,0:T(8,128)(2,1)S(1)}, u32[]{:S(2)}, u32[]{:S(2)}) collective-permute-start(bf16[72,2304]{1,0:T(8,128)(2,1)S(1)} %get-tuple-element.21), channel_id=1, source_target_pairs={{0,2},{1,3},{2,4},{3,5},{4,6},{5,7},{6,0},{7,1},{8,10},{9,11},{10,... | collective-permute-start | bytes 995336 | tf_op jit(solution)/shard_map/ppermute | solution.py:293
Sparse Core Ops, SparseCore 0:
  10.8 103.4 all-gather.1
  162.1 42.0 reduce-scatter.1

commit v4 on v3

--- a/solution.py
+++ b/solution.py
@@ -29,7 +29,7 @@
     return x if amount == 0 else pltpu.roll(x, amount, 1)
 
 
-def pack_kernel(labelled, land_ref, lab_ref, low_ref, high_ref, out_ref, first, second):
+def pack_kernel(counts, land_ref, lab_ref, low_ref, high_ref, early_ref, late_ref, first, second):
     step = pl.program_id(0)
     rows = first.shape[0]
 
@@ -50,39 +50,44 @@
         both = jnp.concatenate([jnp.where(top, a, b), jnp.where(top, b, a)], axis=1)
         return both.reshape(rows * 2, n).astype(jnp.bfloat16)
 
-    if not labelled:
-        out_ref[...] = spread(low_ref[...], high_ref[...])
-        return
-
-    @pl.when(step < pl.num_programs(0) - 1)
-    def _():
-        out_ref[...] = spread(low_ref[...], high_ref[...])
-
-    @pl.when(step == pl.num_programs(0) - 1)
-    def _():
-        out_ref[:, :LANES] = spread(lab_ref[...], lab_ref[...])
-
-
-def pack(land, labels, tiles, devices, first_quad, quads, labelled):
+    @pl.when(step < counts[0])
+    def _():
+        early_ref[...] = spread(low_ref[...], high_ref[...])
+
+    @pl.when(step == counts[0])
+    def _():
+        early_ref[:, :LANES] = spread(lab_ref[...], lab_ref[...])
+
+    @pl.when(step > counts[0])
+    def _():
+        late_ref[...] = spread(low_ref[...], high_ref[...])
+
+
+def pack(land, labels, tiles, devices):
     held = tiles.shape[0]
     block = 768
-    steps = quads * 384 // block
-    at = first_quad * 384 // block
+    counts = [quads * 384 // block for quads in QUADS]
+    source = lambda s: jnp.minimum(s, counts[0] - 1) + jnp.maximum(s - counts[0], 0)
+    rows = devices * 2 * SLOTS
     return pl.pallas_call(
-        functools.partial(pack_kernel, labelled),
-        grid=(steps + int(labelled),),
-        out_shape=jax.ShapeDtypeStruct(
-            (devices * 2 * SLOTS, quads * 384 + LANES * int(labelled)), jnp.bfloat16
-        ),
+        functools.partial(pack_kernel, counts),
+        grid=(sum(counts) + 1,),
+        out_shape=[
+            jax.ShapeDtypeStruct((rows, QUADS[0] * 384 + LANES), jnp.bfloat16),
+            jax.ShapeDtypeStruct((rows, QUADS[1] * 384), jnp.bfloat16),
+        ],
         in_specs=[
             pl.BlockSpec((1, held), lambda s: (0, 0)),
             pl.BlockSpec((held, LANES), lambda s: (0, 0)),
-            pl.BlockSpec((held, block), lambda s: (0, at + jnp.minimum(s, steps - 1))),
-            pl.BlockSpec((held, block), lambda s: (0, at + HALF // block + jnp.minimum(s, steps - 1))),
-        ],
-        out_specs=pl.BlockSpec((devices * 2 * SLOTS, block), lambda s: (0, s)),
+            pl.BlockSpec((held, block), lambda s: (0, source(s))),
+            pl.BlockSpec((held, block), lambda s: (0, HALF // block + source(s))),
+        ],
+        out_specs=[
+            pl.BlockSpec((rows, block), lambda s: (0, jnp.minimum(s, counts[0]))),
+            pl.BlockSpec((rows, block), lambda s: (0, jnp.maximum(s - counts[0] - 1, 0))),
+        ],
         scratch_shapes=[pltpu.VMEM((devices * SLOTS, held), jnp.bfloat16)] * 2,
-        compiler_params=pltpu.CompilerParams(vmem_limit_bytes=56 * MIB),
+        compiler_params=pltpu.CompilerParams(vmem_limit_bytes=58 * MIB),
         name="pack",
     )(land, labels, tiles, tiles)
 
@@ -161,7 +166,7 @@
         ],
         out_specs=pl.BlockSpec((KT * TILE, 4 * TILE), lambda s: (0, s)),
         scratch_shapes=[pltpu.VMEM((JT, KT * TILE, LANES), jnp.bfloat16)],
-        compiler_params=pltpu.CompilerParams(vmem_limit_bytes=40 * MIB),
+        compiler_params=pltpu.CompilerParams(vmem_limit_bytes=38 * MIB),
         name="integrals",
     )(k, j, gathered)
 
@@ -190,91 +195,110 @@
             pl.BlockSpec((rows, LANES), lambda s: (0, labelled.shape[1] // LANES - 1)),
         ],
         out_specs=pl.BlockSpec((2 * VT * KT, rows), lambda s: (0, 0)),
-        compiler_params=pltpu.CompilerParams(vmem_limit_bytes=58 * MIB),
+        compiler_params=pltpu.CompilerParams(vmem_limit_bytes=16 * MIB),
         name="choose",
     )(odd, labelled)
 
 
-def place_kernel(choose_ref, tiles_ref, out_ref):
-    lane = lax.broadcasted_iota(jnp.int32, (48, LANES), 1)
-    lane24 = lax.broadcasted_iota(jnp.int32, (24, LANES), 1)
-    for group in range(2):
-        value = jnp.dot(
-            choose_ref[...],
-            tiles_ref[:, group * 384 : (group + 1) * 384],
-            preferred_element_type=jnp.float32,
-        )
-        for quad in range(KT // 4):
-            pieces = []
-            for b in range(4):
-                rows = value[(quad * 4 + b) * 24 : (quad * 4 + b + 1) * 24]
-                pieces.append(quad_unpack(rows[:, :128], rows[:, 128:256], rows[:, 256:], lane24))
-            base = quad * 384
-            for a in (0, 2):
-                w = [
-                    jnp.concatenate([turn(pieces[b][a + c], 32 * (a + c - b)) for c in range(2)], axis=0)
-                    for b in range(4)
-                ]
-                at = slice((group * 4 + a) * 24, (group * 4 + a) * 24 + 48)
-                out_ref[at, base : base + 128] = jnp.where(lane < 96, w[0], w[1]).astype(jnp.bfloat16)
-                out_ref[at, base + 128 : base + 256] = jnp.where(lane < 64, w[1], w[2]).astype(jnp.bfloat16)
-                out_ref[at, base + 256 : base + 384] = jnp.where(lane < 32, w[2], w[3]).astype(jnp.bfloat16)
-
-
-def place(choose, arrived, quads):
-    return pl.pallas_call(
-        place_kernel,
-        grid=(quads // 2,),
-        out_shape=jax.ShapeDtypeStruct((quads * 96, KT * TILE), jnp.bfloat16),
-        in_specs=[
-            pl.BlockSpec(choose.shape, lambda s: (0, 0)),
-            pl.BlockSpec((arrived.shape[0], 768), lambda s: (0, s)),
-        ],
-        out_specs=pl.BlockSpec((192, KT * TILE), lambda s: (s, 0)),
-        compiler_params=pltpu.CompilerParams(vmem_limit_bytes=58 * MIB),
-        name="place",
-    )(choose, arrived)
-
-
-def product_kernel(from_ref, amp_ref, b_ref, *refs):
-    outs, total = refs[:-1], refs[-1]
+def product_kernel(from_ref, choose_ref, tiles_ref, b_hbm, *refs):
+    outs, (amp, total, b_ref, sems) = refs[:-4], refs[-4:]
+    step = pl.program_id(0)
+    places = amp.shape[0] // 192
+    blocks, _, width = b_ref.shape
+    copies = [
+        pltpu.make_async_copy(b_hbm.at[:, n * width : (n + 1) * width], b_ref.at[n], sems.at[n])
+        for n in range(blocks)
+    ]
+
+    for n in range(blocks):
+
+        @pl.when(step == min(n, places - 1))
+        def _(n=n):
+            copies[n].start()
+
+    for n in range(blocks):
+
+        @pl.when(step == places + n)
+        def _(n=n):
+            copies[n].wait()
+
+    @pl.when(step < places)
+    def _():
+        lane = lax.broadcasted_iota(jnp.int32, (48, LANES), 1)
+        lane24 = lax.broadcasted_iota(jnp.int32, (24, LANES), 1)
+        for group in range(2):
+            value = jnp.dot(
+                choose_ref[...],
+                tiles_ref[:, group * 384 : (group + 1) * 384],
+                preferred_element_type=jnp.float32,
+            )
+            for quad in range(KT // 4):
+                pieces = []
+                for b in range(4):
+                    rows = value[(quad * 4 + b) * 24 : (quad * 4 + b + 1) * 24]
+                    pieces.append(quad_unpack(rows[:, :128], rows[:, 128:256], rows[:, 256:], lane24))
+                base = quad * 384
+                for a in (0, 2):
+                    w = [
+                        jnp.concatenate([turn(pieces[b][a + c], 32 * (a + c - b)) for c in range(2)], axis=0)
+                        for b in range(4)
+                    ]
+                    at = pl.ds(pl.multiple_of(step * 192 + (group * 4 + a) * 24, 48), 48)
+                    amp[at, base : base + 128] = jnp.where(lane < 96, w[0], w[1]).astype(jnp.bfloat16)
+                    amp[at, base + 128 : base + 256] = jnp.where(lane < 64, w[1], w[2]).astype(jnp.bfloat16)
+                    amp[at, base + 256 : base + 384] = jnp.where(lane < 32, w[2], w[3]).astype(jnp.bfloat16)
+
     each = 2 * VT // len(outs)
-    depth = amp_ref.shape[0] // (2 * VT)
+    depth = amp.shape[0] // (2 * VT)
     joined = 1 if depth % 16 == 0 else 2
-    for first in range(0, b_ref.shape[1], 256):
-        value = jnp.dot(amp_ref[...], b_ref[:, first : first + 256], preferred_element_type=jnp.float32)
-        for part in range(2):
-            lanes = slice(first + part * LANES, first + (part + 1) * LANES)
-            slot = first // LANES + part
-            total[slot] = value[:, part * LANES : (part + 1) * LANES]
-            for n, ref in enumerate(outs):
-                for at in range(0, each, joined):
-                    rows = [
-                        total[slot, pl.ds(from_ref[n * each + at + q], depth, stride=2 * VT), :]
-                        for q in range(joined)
-                    ]
-                    ref[at * depth : (at + joined) * depth, lanes] = jnp.concatenate(rows, axis=0).astype(
-                        jnp.bfloat16
-                    )
-
-
-def product(rows_from, amp, integrals, outputs):
+
+    @pl.when(step >= places)
+    def _():
+        for first in range(0, width, 256):
+            value = jnp.dot(
+                amp[...], b_ref[step - places, :, first : first + 256], preferred_element_type=jnp.float32
+            )
+            for part in range(2):
+                lanes = slice(first + part * LANES, first + (part + 1) * LANES)
+                slot = first // LANES + part
+                total[slot] = value[:, part * LANES : (part + 1) * LANES]
+                for n, ref in enumerate(outs):
+                    for at in range(0, each, joined):
+                        rows = [
+                            total[slot, pl.ds(from_ref[n * each + at + q], depth, stride=2 * VT), :]
+                            for q in range(joined)
+                        ]
+                        ref[at * depth : (at + joined) * depth, lanes] = jnp.concatenate(rows, axis=0).astype(
+                            jnp.bfloat16
+                        )
+
+
+def product(rows_from, choose, arrived, quads, integrals, outputs):
     block = 768
-    size = amp.shape[0] // outputs
+    places = quads // 2
+    height = quads * 96
+    size = height // outputs
+    late = lambda s: jnp.maximum(s - places, 0)
     return pl.pallas_call(
         product_kernel,
-        grid=(integrals.shape[1] // block,),
+        grid=(places + integrals.shape[1] // block,),
         out_shape=[jax.ShapeDtypeStruct((size, JT * TILE), jnp.bfloat16)] * outputs,
         in_specs=[
             pl.BlockSpec(memory_space=pltpu.SMEM),
-            pl.BlockSpec(amp.shape, lambda s: (0, 0)),
-            pl.BlockSpec((KT * TILE, block), lambda s: (0, s)),
-        ],
-        out_specs=[pl.BlockSpec((size, block), lambda s: (0, s))] * outputs,
-        scratch_shapes=[pltpu.VMEM((block // LANES, amp.shape[0], LANES), jnp.float32)],
+            pl.BlockSpec(choose.shape, lambda s: (0, 0)),
+            pl.BlockSpec((arrived.shape[0], 768), lambda s: (0, jnp.minimum(s, places - 1))),
+            pl.BlockSpec(memory_space=pl.ANY),
+        ],
+        out_specs=[pl.BlockSpec((size, block), lambda s: (0, late(s)))] * outputs,
+        scratch_shapes=[
+            pltpu.VMEM((height, KT * TILE), jnp.bfloat16),
+            pltpu.VMEM((block // LANES, height, LANES), jnp.float32),
+            pltpu.VMEM((integrals.shape[1] // block, KT * TILE, block), jnp.bfloat16),
+            pltpu.SemaphoreType.DMA((integrals.shape[1] // block,)),
+        ],
         compiler_params=pltpu.CompilerParams(vmem_limit_bytes=58 * MIB),
         name="product",
-    )(rows_from, amp, integrals)
+    )(rows_from, choose, arrived, integrals)
 
 
 def swap_cores(other, own, ctr_count):
@@ -308,10 +332,8 @@
     count = int_rows.shape[1]
     square = int_tiles[0].reshape(count, TILE, TILE).transpose(1, 0, 2).reshape(TILE, count * TILE)
     spare = -(-(count * TILE) // LANES) * LANES - count * TILE
-    int_labels = jnp.pad(
-        jnp.concatenate([int_rows % KT, int_cols], axis=0).astype(jnp.bfloat16),
-        ((0, TILE - 2), (0, spare - count)),
-    )
+    int_names = jnp.concatenate([int_rows, int_cols], axis=0) % KT
+    int_labels = jnp.pad(int_names.astype(jnp.bfloat16), ((0, TILE - 2), (0, spare - count)))
     piece = jnp.concatenate([square, int_labels], axis=1)
     gathered = lax.all_gather(piece, "pair", axis=0, tiled=True)
     target = amp_rows // VT * ctr_count + amp_cols // KT
@@ -320,11 +342,7 @@
     land = target * SLOTS + jnp.sum(earlier.astype(jnp.int32), axis=0)
     labels = lanes_of([amp_cols % KT + 1, amp_rows % VT])
     everyone = ("pair", "ctr")
-    packed = [
-        pack(land[None, :], labels, amp_tiles, devices, sum(QUADS[:n]), quads, n == 0)
-        for n, quads in enumerate(QUADS)
-    ]
-    packed = lax.optimization_barrier(packed)
+    packed = pack(land[None, :], labels, amp_tiles, devices)
     arrived = [
         lax.all_to_all(outgoing, everyone, split_axis=0, concat_axis=0, tiled=True) for outgoing in packed
     ]
@@ -344,12 +362,11 @@
     choose = choosing(odd.reshape(1), arrived[0])
     parts = []
     for n, quads in enumerate(QUADS):
-        amp = place(choose, arrived[n], quads)
         if n < len(QUADS) - 1:
-            [value] = product(natural_rows, amp, integrals, 1)
+            [value] = product(natural_rows, choose, arrived[n], quads, integrals, 1)
             parts.append(lax.psum_scatter(value, "ctr", scatter_dimension=0, tiled=True))
         else:
-            both = swap_cores(*product(spread_rows, amp, integrals, 2), ctr_count)
+            both = swap_cores(*product(spread_rows, choose, arrived[n], quads, integrals, 2), ctr_count)
             parts.append(sum_depths(both, ctr_count))
     parts = [part.reshape(3, quads * 4, -1) for part, quads in zip(parts, QUADS)]
     return jnp.concatenate(parts, axis=1).reshape(144, -1)

time: 236 us -> 230 us (0.975)
  Pallas kernels: 64.4 us -> 52.6 us
  local copies, waits for them, and re-layouts: 5.58 us -> 10.7 us
  waiting for transfers between devices: 37.9 us -> 40.4 us
    pallas_call x6 -> x3, Pallas kernels: 49.9 us -> 42.1 us  [the longest x2 31.9 us: product(): pl.pallas_call(product_kernel, grid=(places + integrals.shape[1] // block...]
    unnamed x6 -> x18, local copies, waits for them, and re-layouts: 2.57 us -> 7.69 us
    all_to_all x1, waiting for transfers between devices: 19.3 us -> 21.8 us  [on_device(): lax.all_to_all(outgoing, everyone, split_axis=0, concat_axis=0, tiled=True)]
  transfers between devices with their start and end apart: 7 -> 7, of which waited for: 5 -> 5; matrix products, arithmetic and copies ran while one was open for 2% -> 2% of each run, Pallas kernels for 28% -> 23%
where the time goes in v4:
time: 230 us; the launch traced here: 228 us
  blocking collectives  94.8 us (41%)
  Pallas kernels  52.6 us (23%)
  waiting for transfers between devices  40.4 us (18%)
  between operations  13.7 us (6%)
  local copies, waits for them, and re-layouts  10.7 us (5%)
  starting transfers between devices  9.23 us (4%)
  other arithmetic  7.12 us (3%)
    all_to_all x1, blocking collectives, on_device(): lax.all_to_all(outgoing, everyone, split_axis=0, concat_axis=0, tiled=True)  94.8 us
    pallas_call x2, Pallas kernels, product(): pl.pallas_call(product_kernel, grid=(places + integrals.shape[1] // block...  31.9 us
    all_to_all x1, waiting for transfers between devices, on_device(): lax.all_to_all(outgoing, everyone, split_axis=0, concat_axis=0, tiled=True)  21.8 us
    ppermute x3, waiting for transfers between devices, sum_depths(): parts.append(lax.ppermute(both[far], 'ctr', move))  15.2 us
    pallas_call x1, Pallas kernels, pack(): pl.pallas_call(functools.partial(pack_kernel, counts), grid=(sum(counts)...  10.2 us
    pallas_call x1, Pallas kernels, place_integrals(): pl.pallas_call(integral_kernel, grid=(JT // 4,), out_shape=jax.ShapeDtype...  9.79 us
    unnamed x18, local copies, waits for them, and re-layouts  7.69 us
    all_to_all x1, starting transfers between devices, on_device(): lax.all_to_all(outgoing, everyone, split_axis=0, concat_axis=0, tiled=True)  5.78 us
  transfers between devices with their start and end apart: 7, of which 5 were waited for; matrix products, arithmetic and copies ran while one was open for 2% of the time, Pallas kernels for 23%

profile of v4, /device:TPU:0, one launch (start us, length us, event | category | flops | bytes accessed | tf_op | source)
XLA Modules:
  0.0 228.5 jit_solution(4313945592483888371)
XLA Ops:
  6.5 1.5 reshape_squeeze.9
  8.1 0.3 copy.16
  8.3 0.2 copy.17
  8.6 0.8 fusion.1
  9.5 0.1 copy.15
  9.6 0.6 pad.8.lab_ref
  10.3 0.1 convert_reduce_fusion
  10.4 0.5 multiply_add_fusion
  10.9 10.2 %pack.1 = (bf16[1024,2432]{1,0:T(8,128)(2,1)}, bf16[1024,2304]{1,0:T(8,128)(2,1)}) custom-call(s32[1,256]{1,0:T(1,128)} %bitcast.23, bf16[256,128]{1,0:T(8,128)(2,1)} %pad.8.lab_ref, bf16[256,9216]{1,0:T(8,128)(2,1)} %high_ref.1, bf16[256,9216]{1,0:T(8,128)(2,1)} %high_ref.1), custom_call_target="tpu_custom_call" | custom-call | tf_op jit(solution)/shard_map/pack/pallas_call | solution.py:72
  21.1 94.8 %all_to_all.23 = bf16[128,8,2432]{2,1,0:T(8,128)(2,1)} all-to-all(bf16[128,8,2432]{2,1,0:T(8,128)(2,1)} %bitcast.18), channel_id=1, replica_groups=mesh['pair'=16,'ctr'=8] {'pair','ctr'}, dimensions={0} | all-to-all | bytes 9961472 | tf_op jit(solution)/shard_map/all_to_all | solution.py:347
  115.9 5.8 %all-to-all-start.1 = ((bf16[128,8,2304]{2,1,0:T(8,128)(2,1)}), bf16[128,8,2304]{2,1,0:T(8,128)(2,1)}, u32[]{:S(2)}, u32[]{:S(2)}) async-start(bf16[128,8,2304]{2,1,0:T(8,128)(2,1)} %bitcast.19), calls=%async_computation.2 | async-start | bytes 9437184 | tf_op jit(solution)/shard_map/all_to_all | solution.py:347
  121.8 0.5 fusion.9.from_ref
  122.3 0.8 slice_convert_fusion
  123.2 0.1 reshape_squeeze.11.j_ref
  123.4 2.6 %copy-done.2 = bf16[1536,1792]{1,0:T(8,128)(2,1)S(1)} copy-done((bf16[1536,1792]{1,0:T(8,128)(2,1)S(1)}, bf16[1536,1792]{1,0:T(8,128)(2,1)}, u32[]{:S(2)}) %copy-start.2) | copy-done | bytes 5505048
  126.0 9.8 %integrals.1.b_hbm = bf16[2304,2304]{1,0:T(8,128)(2,1)S(1)} custom-call(s32[288]{0:T(512)S(1)} %reshape_squeeze.10.k_ref, s32[288]{0:T(512)S(1)} %reshape_squeeze.11.j_ref, bf16[1536,1792]{1,0:T(8,128)(2,1)S(1)} %copy-done.2), custom_call_target="tpu_custom_call" | custom-call | tf_op jit(solution)/shard_map/integrals/pallas_call | solution.py:158
  135.8 4.0 %copy-done = bf16[2304,2304]{1,0:T(8,128)(2,1)} copy-done((bf16[2304,2304]{1,0:T(8,128)(2,1)}, bf16[2304,2304]{1,0:T(8,128)(2,1)S(1)}, u32[]{:S(2)}) %copy-start) | copy-done | bytes 10616856
  139.9 0.7 choose.1.choose_ref
  140.6 1.0 copy-done.1
  141.6 15.9 %product.2 = bf16[576,2304]{1,0:T(8,128)(2,1)} custom-call(s32[24]{0:T(128)} %fusion.9.from_ref, bf16[576,1024]{1,0:T(8,128)(2,1)} %copy-done.1, bf16[1024,2432]{1,0:T(8,128)(2,1)} %bitcast.13, bf16[2304,2304]{1,0:T(8,128)(2,1)} %copy-done), custom_call_target="tpu_custom_call" | custom-call | tf_op jit(solution)/shard_map/product/pallas_call | solution.py:282
  157.6 0.6 fusion.14.from_ref
  158.1 21.8 %all-to-all-done.1 = bf16[128,8,2304]{2,1,0:T(8,128)(2,1)} async-done(((bf16[128,8,2304]{2,1,0:T(8,128)(2,1)}), bf16[128,8,2304]{2,1,0:T(8,128)(2,1)}, u32[]{:S(2)}, u32[]{:S(2)}) %all-to-all-start.1) | async-done | bytes 4718624 | tf_op jit(solution)/shard_map/all_to_all | solution.py:347
  180.0 16.0 %product.3 = (bf16[288,2304]{1,0:T(8,128)(2,1)}, bf16[288,2304]{1,0:T(8,128)(2,1)}) custom-call(s32[24]{0:T(128)} %fusion.14.from_ref, bf16[576,1024]{1,0:T(8,128)(2,1)} %copy-done.1, bf16[1024,2304]{1,0:T(8,128)(2,1)} %bitcast.9.tiles_ref, bf16[2304,2304]{1,0:T(8,128)(2,1)} %copy-done), custom_call_target="tpu_custom_call" | custom-call | tf_op jit(solution)/shard_map/product/pallas_call | solution.py:282
  196.0 3.3 %collective-permute-done = bf16[288,2304]{1,0:T(8,128)(2,1)S(1)} collective-permute-done((bf16[288,2304]{1,0:T(8,128)(2,1)}, bf16[288,2304]{1,0:T(8,128)(2,1)S(1)}, u32[]{:S(2)}, u32[]{:S(2)}) %collective-permute-start) | collective-permute-done | bytes 1327136 | tf_op jit(solution)/shard_map/ppermute | solution.py:306
  199.3 1.7 add_convert_fusion
  201.1 0.3 collective-permute-start.1
  201.4 3.0 %collective-permute-start.3 = (bf16[72,2304]{1,0:T(8,128)(2,1)S(1)}, bf16[72,2304]{1,0:T(8,128)(2,1)S(1)}, u32[]{:S(2)}, u32[]{:S(2)}) collective-permute-start(bf16[72,2304]{1,0:T(8,128)(2,1)S(1)} %get-tuple-element.20), channel_id=1, source_target_pairs={{0,6},{1,7},{2,0},{3,1},{4,2},{5,3},{6,4},{7,5},{8,14},{9,15},{10,... | collective-permute-start | bytes 995336 | tf_op jit(solution)/shard_map/ppermute | solution.py:317
  204.4 8.9 %collective-permute-done.1 = bf16[72,2304]{1,0:T(8,128)(2,1)S(1)} collective-permute-done((bf16[72,2304]{1,0:T(8,128)(2,1)S(1)}, bf16[72,2304]{1,0:T(8,128)(2,1)S(1)}, u32[]{:S(2)}, u32[]{:S(2)}) %collective-permute-start.1) | collective-permute-done | bytes 331808 | tf_op jit(solution)/shard_map/ppermute | solution.py:317
  213.3 3.8 %collective-permute-done.3 = bf16[72,2304]{1,0:T(8,128)(2,1)S(1)} collective-permute-done((bf16[72,2304]{1,0:T(8,128)(2,1)S(1)}, bf16[72,2304]{1,0:T(8,128)(2,1)S(1)}, u32[]{:S(2)}, u32[]{:S(2)}) %collective-permute-start.3) | collective-permute-done | bytes 331808 | tf_op jit(solution)/shard_map/ppermute | solution.py:317
  217.1 2.5 %collective-permute-done.2 = bf16[72,2304]{1,0:T(8,128)(2,1)S(1)} collective-permute-done((bf16[72,2304]{1,0:T(8,128)(2,1)S(1)}, bf16[72,2304]{1,0:T(8,128)(2,1)S(1)}, u32[]{:S(2)}, u32[]{:S(2)}) %collective-permute-start.2) | collective-permute-done | bytes 331808 | tf_op jit(solution)/shard_map/ppermute | solution.py:317
  219.6 0.2 add_convert_fusion.1
  219.8 1.9 pad_maximum_fusion
  (32 shorter events, 0.5 us)
Async XLA Ops:
  6.5 2.0 copy-start.5
  6.5 2.0 copy-start.6
  6.5 115.8 %all-gather.2.cloned.1.call-start = ((), (), s32[]{:S(2)}) async-start(), calls=%async_computation.3 | async-start | bytes 5849088 | tf_op jit(solution)/shard_map/all_gather | solution.py:338
  8.0 1.4 copy-start.3
  8.1 1.4 copy-start.4
  115.9 64.0 %all-to-all-start.1 = ((bf16[128,8,2304]{2,1,0:T(8,128)(2,1)}), bf16[128,8,2304]{2,1,0:T(8,128)(2,1)}, u32[]{:S(2)}, u32[]{:S(2)}) async-start(bf16[128,8,2304]{2,1,0:T(8,128)(2,1)} %bitcast.19), calls=%async_computation.2 | async-start | bytes 9437184 | tf_op jit(solution)/shard_map/all_to_all | solution.py:347
  121.7 98.1 %reduce-scatter.2.cloned.1.call-start = ((), (), s32[]{:S(2)}) async-start(), calls=%async_computation.4 | async-start | bytes 2985984 | tf_op jit(solution)/shard_map/reduce_scatter | solution.py:367
  123.3 16.6 %slice-start = ((s8[4980736]{0:T(1024)(128)(4,1)}), s8[786432]{0:T(1024)(128)(4,1)S(1)}, s32[]{:S(2)}) async-start(s8[4980736]{0:T(1024)(128)(4,1)} %bitcast.14), calls=%async_computation.5 | async-start | bytes 1572864
  123.4 2.6 %copy-start.2 = (bf16[1536,1792]{1,0:T(8,128)(2,1)S(1)}, bf16[1536,1792]{1,0:T(8,128)(2,1)}, u32[]{:S(2)}) copy-start(bf16[1536,1792]{1,0:T(8,128)(2,1)} %all-gather.2.cloned.1.call-done.tiles_ref) | copy-start | bytes 16515076
  126.0 13.9 %slice-start.1 = ((s8[4980736]{0:T(1024)(128)(4,1)}), s8[4194304]{0:T(1024)(128)(4,1)S(1)}, s32[]{:S(2)}) async-start(s8[4980736]{0:T(1024)(128)(4,1)} %bitcast.14), calls=%async_computation.6 | async-start | bytes 8388608
  135.8 4.0 %copy-start = (bf16[2304,2304]{1,0:T(8,128)(2,1)}, bf16[2304,2304]{1,0:T(8,128)(2,1)S(1)}, u32[]{:S(2)}) copy-start(bf16[2304,2304]{1,0:T(8,128)(2,1)S(1)} %integrals.1.b_hbm) | copy-start | bytes 31850500
  140.5 1.0 copy-start.1
  196.0 3.3 %collective-permute-start = (bf16[288,2304]{1,0:T(8,128)(2,1)}, bf16[288,2304]{1,0:T(8,128)(2,1)S(1)}, u32[]{:S(2)}, u32[]{:S(2)}) collective-permute-start(bf16[288,2304]{1,0:T(8,128)(2,1)} %get-tuple-element.16), channel_id=1, source_target_pairs={{0,1},{1,0},{2,3},{3,2},{4,5},{5,4},{6,7},{7,6},{8,9},{9,8},{10,11... | collective-permute-start | bytes 3981320 | tf_op jit(solution)/shard_map/ppermute | solution.py:306
  201.1 12.3 %collective-permute-start.1 = (bf16[72,2304]{1,0:T(8,128)(2,1)S(1)}, bf16[72,2304]{1,0:T(8,128)(2,1)S(1)}, u32[]{:S(2)}, u32[]{:S(2)}) collective-permute-start(bf16[72,2304]{1,0:T(8,128)(2,1)S(1)} %get-tuple-element.19), channel_id=1, source_target_pairs={{0,4},{1,5},{2,6},{3,7},{4,0},{5,1},{6,2},{7,3},{8,12},{9,13},{10,... | collective-permute-start | bytes 995336 | tf_op jit(solution)/shard_map/ppermute | solution.py:317
  201.4 15.7 %collective-permute-start.3 = (bf16[72,2304]{1,0:T(8,128)(2,1)S(1)}, bf16[72,2304]{1,0:T(8,128)(2,1)S(1)}, u32[]{:S(2)}, u32[]{:S(2)}) collective-permute-start(bf16[72,2304]{1,0:T(8,128)(2,1)S(1)} %get-tuple-element.20), channel_id=1, source_target_pairs={{0,6},{1,7},{2,0},{3,1},{4,2},{5,3},{6,4},{7,5},{8,14},{9,15},{10,... | collective-permute-start | bytes 995336 | tf_op jit(solution)/shard_map/ppermute | solution.py:317
  204.4 15.2 %collective-permute-start.2 = (bf16[72,2304]{1,0:T(8,128)(2,1)S(1)}, bf16[72,2304]{1,0:T(8,128)(2,1)S(1)}, u32[]{:S(2)}, u32[]{:S(2)}) collective-permute-start(bf16[72,2304]{1,0:T(8,128)(2,1)S(1)} %get-tuple-element.21), channel_id=1, source_target_pairs={{0,2},{1,3},{2,4},{3,5},{4,6},{5,7},{6,0},{7,1},{8,10},{9,11},{10,... | collective-permute-start | bytes 995336 | tf_op jit(solution)/shard_map/ppermute | solution.py:317
Sparse Core Ops, SparseCore 0:
  9.5 102.7 all-gather.1
  157.7 44.4 reduce-scatter.1

commit v5 on v4

--- a/solution.py
+++ b/solution.py
@@ -17,7 +17,7 @@
 SLOTS = 4
 LANES = 128
 MIB = 2**20
-QUADS = (6, 6)
+QUADS = (8, 4)
 
 
 def quad_unpack(v0, v1, v2, lane):
@@ -105,17 +105,21 @@
     )
 
 
-def integral_kernel(k_ref, j_ref, tiles_ref, out_ref, spread):
+def integral_kernel(names_ref, tiles_hbm, out_ref, tiles_ref, spread, sem):
     step = pl.program_id(0)
-    held = (tiles_ref.shape[1] - 1) // TILE
+    sources, _, held = names_ref.shape
 
     @pl.when(step == 0)
     def _():
+        copy = pltpu.make_async_copy(tiles_hbm, tiles_ref, sem)
+        copy.start()
+
         def clear(at, carry):
             spread[at] = jnp.zeros(spread.shape[1:], spread.dtype)
             return carry
 
         lax.fori_loop(0, JT, clear, 0)
+        copy.wait()
         lane = lax.broadcasted_iota(jnp.int32, (TILE, LANES), 1)
 
         def source(at, carry):
@@ -130,15 +134,15 @@
                 v = [v[0] if x is None else x for x in v]
                 pieces = quad_unpack(*v, lane)
                 for a in range(min(4, held - quad * 4)):
-                    k = k_ref[at * held + quad * 4 + a]
-                    j = j_ref[at * held + quad * 4 + a]
+                    k = names_ref[at, 0, quad * 4 + a]
+                    j = names_ref[at, 1, quad * 4 + a]
                     amount = (32 * a + 96 * (j % 4)) % LANES
                     spread[j, pl.ds(pl.multiple_of(k * TILE, TILE), TILE), :] = pltpu.roll(
                         pieces[a], amount, 1
                     ).astype(jnp.bfloat16)
             return carry
 
-        lax.fori_loop(0, tiles_ref.shape[0] // TILE, source, 0)
+        lax.fori_loop(0, sources, source, 0)
 
     size = 256
 
@@ -154,62 +158,57 @@
     lax.fori_loop(0, KT * TILE // size, join, 0)
 
 
-def place_integrals(k, j, gathered):
+def place_integrals(names, gathered):
     return pl.pallas_call(
         integral_kernel,
         grid=(JT // 4,),
         out_shape=jax.ShapeDtypeStruct((KT * TILE, JT * TILE), jnp.bfloat16),
         in_specs=[
             pl.BlockSpec(memory_space=pltpu.SMEM),
-            pl.BlockSpec(memory_space=pltpu.SMEM),
-            pl.BlockSpec(gathered.shape, lambda s: (0, 0)),
+            pl.BlockSpec(memory_space=pl.ANY),
         ],
         out_specs=pl.BlockSpec((KT * TILE, 4 * TILE), lambda s: (0, s)),
-        scratch_shapes=[pltpu.VMEM((JT, KT * TILE, LANES), jnp.bfloat16)],
-        compiler_params=pltpu.CompilerParams(vmem_limit_bytes=38 * MIB),
+        scratch_shapes=[
+            pltpu.VMEM(gathered.shape, jnp.bfloat16),
+            pltpu.VMEM((JT, KT * TILE, LANES), jnp.bfloat16),
+            pltpu.SemaphoreType.DMA,
+        ],
+        compiler_params=pltpu.CompilerParams(vmem_limit_bytes=60 * MIB),
         name="integrals",
-    )(k, j, gathered)
-
-
-def choose_kernel(odd_ref, lab_ref, choose_ref):
-    labels = label_rows(lab_ref[...])
-    column = lax.broadcasted_iota(jnp.int32, (1, lab_ref.shape[0]), 1)
-    second = ((column & SLOTS) // SLOTS) ^ odd_ref[0]
-    k = labels[0:1].astype(jnp.int32) - 1
-    i = labels[1:2].astype(jnp.int32)
-    cell = k * (2 * VT) + second * VT + i
-    row = lax.broadcasted_iota(jnp.int32, choose_ref.shape, 0)
-    choose_ref[...] = jnp.where(row == jnp.broadcast_to(cell, choose_ref.shape), 1.0, 0.0).astype(
-        jnp.bfloat16
-    )
-
-
-def choosing(odd, labelled):
-    rows = labelled.shape[0]
-    return pl.pallas_call(
-        choose_kernel,
-        grid=(1,),
-        out_shape=jax.ShapeDtypeStruct((2 * VT * KT, rows), jnp.bfloat16),
-        in_specs=[
-            pl.BlockSpec(memory_space=pltpu.SMEM),
-            pl.BlockSpec((rows, LANES), lambda s: (0, labelled.shape[1] // LANES - 1)),
-        ],
-        out_specs=pl.BlockSpec((2 * VT * KT, rows), lambda s: (0, 0)),
-        compiler_params=pltpu.CompilerParams(vmem_limit_bytes=16 * MIB),
-        name="choose",
-    )(odd, labelled)
-
-
-def product_kernel(from_ref, choose_ref, tiles_ref, b_hbm, *refs):
-    outs, (amp, total, b_ref, sems) = refs[:-4], refs[-4:]
+    )(names, gathered)
+
+
+def product_kernel(depths, ctr_ref, lab_ref, tiles_ref, b_hbm, *refs):
+    outs, (choose, amp, total, b_ref, sems) = refs[:-5], refs[-5:]
     step = pl.program_id(0)
     places = amp.shape[0] // 192
     blocks, _, width = b_ref.shape
+    odd, layer = ctr_ref[0] & 1, ctr_ref[0] >> 1
     copies = [
         pltpu.make_async_copy(b_hbm.at[:, n * width : (n + 1) * width], b_ref.at[n], sems.at[n])
         for n in range(blocks)
     ]
 
+    def row_of(n, at):
+        block = at
+        if len(outs) == 2:
+            core = odd if n == 1 else 1 - odd
+            block = ((layer + at // 3) % depths * 2 + core) * 3 + at % 3
+        return (block & 1) * VT + (block >> 1)
+
+    @pl.when(step == 0)
+    def _():
+        labels = label_rows(lab_ref[...])
+        column = lax.broadcasted_iota(jnp.int32, (1, lab_ref.shape[0]), 1)
+        second = ((column & SLOTS) // SLOTS) ^ odd
+        k = labels[0:1].astype(jnp.int32) - 1
+        i = labels[1:2].astype(jnp.int32)
+        cell = k * (2 * VT) + second * VT + i
+        row = lax.broadcasted_iota(jnp.int32, choose.shape, 0)
+        choose[...] = jnp.where(row == jnp.broadcast_to(cell, choose.shape), 1.0, 0.0).astype(
+            jnp.bfloat16
+        )
+
     for n in range(blocks):
 
         @pl.when(step == min(n, places - 1))
@@ -228,7 +227,7 @@
         lane24 = lax.broadcasted_iota(jnp.int32, (24, LANES), 1)
         for group in range(2):
             value = jnp.dot(
-                choose_ref[...],
+                choose[...],
                 tiles_ref[:, group * 384 : (group + 1) * 384],
                 preferred_element_type=jnp.float32,
             )
@@ -265,7 +264,7 @@
                 for n, ref in enumerate(outs):
                     for at in range(0, each, joined):
                         rows = [
-                            total[slot, pl.ds(from_ref[n * each + at + q], depth, stride=2 * VT), :]
+                            total[slot, pl.ds(row_of(n, at + q), depth, stride=2 * VT), :]
                             for q in range(joined)
                         ]
                         ref[at * depth : (at + joined) * depth, lanes] = jnp.concatenate(rows, axis=0).astype(
@@ -273,32 +272,37 @@
                         )
 
 
-def product(rows_from, choose, arrived, quads, integrals, outputs):
+def product(ctr, labelled, arrived, quads, integrals, outputs, depths):
     block = 768
+    blocks = integrals.shape[1] // block
     places = quads // 2
     height = quads * 96
     size = height // outputs
+    rows = arrived.shape[0]
+    flops = 10**6 if outputs == 1 else 10**11
     late = lambda s: jnp.maximum(s - places, 0)
     return pl.pallas_call(
-        product_kernel,
-        grid=(places + integrals.shape[1] // block,),
+        functools.partial(product_kernel, depths),
+        grid=(places + blocks,),
         out_shape=[jax.ShapeDtypeStruct((size, JT * TILE), jnp.bfloat16)] * outputs,
         in_specs=[
             pl.BlockSpec(memory_space=pltpu.SMEM),
-            pl.BlockSpec(choose.shape, lambda s: (0, 0)),
-            pl.BlockSpec((arrived.shape[0], 768), lambda s: (0, jnp.minimum(s, places - 1))),
+            pl.BlockSpec((rows, LANES), lambda s: (0, labelled.shape[1] // LANES - 1)),
+            pl.BlockSpec((rows, 768), lambda s: (0, jnp.minimum(s, places - 1))),
             pl.BlockSpec(memory_space=pl.ANY),
         ],
         out_specs=[pl.BlockSpec((size, block), lambda s: (0, late(s)))] * outputs,
         scratch_shapes=[
+            pltpu.VMEM((2 * VT * KT, rows), jnp.bfloat16),
             pltpu.VMEM((height, KT * TILE), jnp.bfloat16),
             pltpu.VMEM((block // LANES, height, LANES), jnp.float32),
-            pltpu.VMEM((integrals.shape[1] // block, KT * TILE, block), jnp.bfloat16),
-            pltpu.SemaphoreType.DMA((integrals.shape[1] // block,)),
-        ],
-        compiler_params=pltpu.CompilerParams(vmem_limit_bytes=58 * MIB),
+            pltpu.VMEM((blocks, KT * TILE, block), jnp.bfloat16),
+            pltpu.SemaphoreType.DMA((blocks,)),
+        ],
+        compiler_params=pltpu.CompilerParams(vmem_limit_bytes=61 * MIB),
+        cost_estimate=pl.CostEstimate(flops=flops, bytes_accessed=flops // 300, transcendentals=0),
         name="product",
-    )(rows_from, choose, arrived, integrals)
+    )(ctr, labelled, arrived, integrals)
 
 
 def swap_cores(other, own, ctr_count):
@@ -346,27 +350,19 @@
     arrived = [
         lax.all_to_all(outgoing, everyone, split_axis=0, concat_axis=0, tiled=True) for outgoing in packed
     ]
-    ctr = lax.axis_index("ctr").astype(jnp.int32)
-    odd, depth = ctr % 2, ctr // 2
-    which = jnp.arange(2 * VT, dtype=jnp.int32)
-    core = jnp.where(which < VT, 1 - odd, odd)
-    owner = (depth + which % VT // 3) % (ctr_count // 2) * 2 + core
-    block = 3 * owner + which % 3
-    spread_rows = block % 2 * VT + block // 2
-    block = jnp.arange(2 * VT, dtype=jnp.int32)
-    natural_rows = block % 2 * VT + block // 2
+    ctr = lax.axis_index("ctr").astype(jnp.int32).reshape(1)
     names = gathered.reshape(-1, TILE, piece.shape[1])[:, :2, count * TILE : count * TILE + count]
-    names = names.astype(jnp.int32)
-    integrals = place_integrals(names[:, 0].reshape(-1), names[:, 1].reshape(-1), gathered)
+    integrals = place_integrals(names.astype(jnp.int32), gathered)
     arrived[0], integrals = lax.optimization_barrier((arrived[0], integrals))
-    choose = choosing(odd.reshape(1), arrived[0])
     parts = []
     for n, quads in enumerate(QUADS):
         if n < len(QUADS) - 1:
-            [value] = product(natural_rows, choose, arrived[n], quads, integrals, 1)
+            [value] = product(ctr, arrived[0], arrived[n], quads, integrals, 1, ctr_count // 2)
             parts.append(lax.psum_scatter(value, "ctr", scatter_dimension=0, tiled=True))
         else:
-            both = swap_cores(*product(spread_rows, choose, arrived[n], quads, integrals, 2), ctr_count)
+            both = swap_cores(
+                *product(ctr, arrived[0], arrived[n], quads, integrals, 2, ctr_count // 2), ctr_count
+            )
             parts.append(sum_depths(both, ctr_count))
     parts = [part.reshape(3, quads * 4, -1) for part, quads in zip(parts, QUADS)]
     return jnp.concatenate(parts, axis=1).reshape(144, -1)

time: 230 us -> 228 us (level)
  blocking collectives: 94.8 us -> 112 us
  waiting for transfers between devices: 40.4 us -> 29 us
  local copies, waits for them, and re-layouts: 10.7 us -> 2.8 us
    all_to_all x1, blocking collectives: 94.8 us -> 112 us  [on_device(): lax.all_to_all(outgoing, everyone, split_axis=0, concat_axis=0, tiled=True)]
    all_to_all x1, waiting for transfers between devices: 21.8 us -> 7.65 us  [on_device(): lax.all_to_all(outgoing, everyone, split_axis=0, concat_axis=0, tiled=True)]
    unnamed x18 -> x4, local copies, waits for them, and re-layouts: 7.69 us -> 0.01 us
    reduce_scatter x1, waiting for transfers between devices: 0.02 us -> 5.43 us  [on_device(): lax.psum_scatter(value, 'ctr', scatter_dimension=0, tiled=True)]
    pallas_call x1, Pallas kernels: 9.79 us -> 12.9 us  [place_integrals(): pl.pallas_call(integral_kernel, grid=(JT // 4,), out_shape=jax.ShapeDtype...]
    pallas_call x3 -> x2, Pallas kernels: 32.6 us -> 31.1 us  [product(): pl.pallas_call(functools.partial(product_kernel, depths), grid=(places +...]
  transfers between devices with their start and end apart: 7 -> 7, of which waited for: 5 -> 6; matrix products, arithmetic and copies ran while one was open for 2% -> 2% of each run, Pallas kernels for 23% -> 24%
where the time goes in v5:
time: 228 us; the launch traced here: 226 us
  blocking collectives  112 us (49%)
  Pallas kernels  53.2 us (23%)
  waiting for transfers between devices  29 us (13%)
  between operations  13.5 us (6%)
  starting transfers between devices  9.26 us (4%)
  other arithmetic  7.03 us (3%)
  local copies, waits for them, and re-layouts  2.8 us (1%)
    all_to_all x1, blocking collectives, on_device(): lax.all_to_all(outgoing, everyone, split_axis=0, concat_axis=0, tiled=True)  112 us
    pallas_call x2, Pallas kernels, product(): pl.pallas_call(functools.partial(product_kernel, depths), grid=(places +...  31.1 us
    ppermute x3, waiting for transfers between devices, sum_depths(): parts.append(lax.ppermute(both[far], 'ctr', move))  13.3 us
    pallas_call x1, Pallas kernels, place_integrals(): pl.pallas_call(integral_kernel, grid=(JT // 4,), out_shape=jax.ShapeDtype...  12.9 us
    pallas_call x1, Pallas kernels, pack(): pl.pallas_call(functools.partial(pack_kernel, counts), grid=(sum(counts)...  9.26 us
    all_to_all x1, waiting for transfers between devices, on_device(): lax.all_to_all(outgoing, everyone, split_axis=0, concat_axis=0, tiled=True)  7.65 us
    all_to_all x1, starting transfers between devices, on_device(): lax.all_to_all(outgoing, everyone, split_axis=0, concat_axis=0, tiled=True)  5.74 us
    reduce_scatter x1, waiting for transfers between devices, on_device(): lax.psum_scatter(value, 'ctr', scatter_dimension=0, tiled=True)  5.43 us
  transfers between devices with their start and end apart: 7, of which 6 were waited for; matrix products, arithmetic and copies ran while one was open for 2% of the time, Pallas kernels for 24%

profile of v5, /device:TPU:0, one launch (start us, length us, event | category | flops | bytes accessed | tf_op | source)
XLA Modules:
  0.0 226.4 jit_solution(1833842555615973688)
XLA Ops:
  6.5 1.5 reshape_squeeze.3
  8.0 0.3 copy.16
  8.3 0.2 copy.17
  8.5 0.7 fusion.6
  9.2 0.8 fusion.1
  10.1 0.1 copy.15
  10.3 0.6 pad.8.lab_ref
  10.9 0.1 convert_reduce_fusion
  11.0 0.5 multiply_add_fusion
  11.5 9.3 %pack.1 = (bf16[1024,3200]{1,0:T(8,128)(2,1)}, bf16[1024,1536]{1,0:T(8,128)(2,1)}) custom-call(s32[1,256]{1,0:T(1,128)} %bitcast.21, bf16[256,128]{1,0:T(8,128)(2,1)} %pad.8.lab_ref, bf16[256,9216]{1,0:T(8,128)(2,1)} %high_ref.1, bf16[256,9216]{1,0:T(8,128)(2,1)} %high_ref.1), custom_call_target="tpu_custom_call" | custom-call | tf_op jit(solution)/shard_map/pack/pallas_call | solution.py:72
  20.8 111.6 %all_to_all.23 = bf16[128,8,3200]{2,1,0:T(8,128)(2,1)} all-to-all(bf16[128,8,3200]{2,1,0:T(8,128)(2,1)} %bitcast.16), channel_id=1, replica_groups=mesh['pair'=16,'ctr'=8] {'pair','ctr'}, dimensions={0} | all-to-all | bytes 13107200 | tf_op jit(solution)/shard_map/all_to_all | solution.py:351
  132.4 5.7 %all-to-all-start.1 = ((bf16[128,8,1536]{2,1,0:T(8,128)(2,1)}), bf16[128,8,1536]{2,1,0:T(8,128)(2,1)}, u32[]{:S(2)}, u32[]{:S(2)}) async-start(bf16[128,8,1536]{2,1,0:T(8,128)(2,1)} %bitcast.8), calls=%async_computation.2 | async-start | bytes 6291456 | tf_op jit(solution)/shard_map/all_to_all | solution.py:351
  138.1 0.0 reduce-scatter.2.cloned.1.call-start
  138.2 0.0 all-gather.2.cloned.1.call-done.tiles_hbm
  138.2 1.4 slice_convert_fusion.names_ref
  139.7 12.9 %integrals.1.b_hbm = bf16[2304,2304]{1,0:T(8,128)(2,1)} custom-call(s32[16,2,18]{2,1,0:T(2,128)} %slice_convert_fusion.names_ref, bf16[1536,1792]{1,0:T(8,128)(2,1)} %all-gather.2.cloned.1.call-done.tiles_hbm), custom_call_target="tpu_custom_call" | custom-call | tf_op jit(solution)/shard_map/integrals/pallas_call | solution.py:162
  152.6 19.2 %product.2 = bf16[768,2304]{1,0:T(8,128)(2,1)} custom-call(s32[1]{0:T(128)} %bitcast.ctr_ref, bf16[1024,3200]{1,0:T(8,128)(2,1)} %bitcast.13, bf16[1024,3200]{1,0:T(8,128)(2,1)} %bitcast.14, bf16[2304,2304]{1,0:T(8,128)(2,1)} %integrals.1.b_hbm), custom_call_target="tpu_custom_call" | custom-call | flops 1000000 | bytes 3333 | tf_op jit(solution)/shard_map/product/pallas_call | solution.py:284
  171.7 0.0 reduce-scatter.2.cloned.1.call-update
  171.8 7.7 %all-to-all-done.1 = bf16[128,8,1536]{2,1,0:T(8,128)(2,1)} async-done(((bf16[128,8,1536]{2,1,0:T(8,128)(2,1)}), bf16[128,8,1536]{2,1,0:T(8,128)(2,1)}, u32[]{:S(2)}, u32[]{:S(2)}) %all-to-all-start.1) | async-done | bytes 3145760 | tf_op jit(solution)/shard_map/all_to_all | solution.py:351
  179.4 11.9 %product.3 = (bf16[192,2304]{1,0:T(8,128)(2,1)}, bf16[192,2304]{1,0:T(8,128)(2,1)}) custom-call(s32[1]{0:T(128)} %bitcast.ctr_ref, bf16[1024,3200]{1,0:T(8,128)(2,1)} %bitcast.15, bf16[1024,1536]{1,0:T(8,128)(2,1)} %bitcast.9.tiles_ref, bf16[2304,2304]{1,0:T(8,128)(2,1)} %integrals.1.b_hbm), custom_call_target="tpu_custom_call" | custom-call | flops 99999997952 | bytes 333333344 | tf_op jit(solution)/shard_map/product/pallas_call | solution.py:284
  191.3 0.1 collective-permute-start
  191.4 2.6 %collective-permute-done = bf16[192,2304]{1,0:T(8,128)(2,1)S(1)} collective-permute-done((bf16[192,2304]{1,0:T(8,128)(2,1)}, bf16[192,2304]{1,0:T(8,128)(2,1)S(1)}, u32[]{:S(2)}, u32[]{:S(2)}) %collective-permute-start) | collective-permute-done | bytes 884768 | tf_op jit(solution)/shard_map/ppermute | solution.py:310
  194.0 1.4 add_convert_fusion
  195.5 0.1 collective-permute-start.1
  195.6 1.3 collective-permute-start.2
  196.9 2.0 collective-permute-start.3
  198.9 8.8 %collective-permute-done.1 = bf16[48,2304]{1,0:T(8,128)(2,1)S(1)} collective-permute-done((bf16[48,2304]{1,0:T(8,128)(2,1)S(1)}, bf16[48,2304]{1,0:T(8,128)(2,1)S(1)}, u32[]{:S(2)}, u32[]{:S(2)}) %collective-permute-start.1) | collective-permute-done | bytes 221216 | tf_op jit(solution)/shard_map/ppermute | solution.py:321
  207.7 3.9 %collective-permute-done.2 = bf16[48,2304]{1,0:T(8,128)(2,1)S(1)} collective-permute-done((bf16[48,2304]{1,0:T(8,128)(2,1)S(1)}, bf16[48,2304]{1,0:T(8,128)(2,1)S(1)}, u32[]{:S(2)}, u32[]{:S(2)}) %collective-permute-start.2) | collective-permute-done | bytes 221216 | tf_op jit(solution)/shard_map/ppermute | solution.py:321
  211.7 0.5 collective-permute-done.3
  212.2 0.1 add_convert_fusion.1
  212.3 5.4 %reduce-scatter.2.cloned.1.call-done = bf16[96,2304]{1,0:T(8,128)(2,1)} async-done(((bf16[768,2304]{1,0:T(8,128)(2,1)}), bf16[96,2304]{1,0:T(8,128)(2,1)}) %reduce-scatter.2.cloned.1.call-update) | async-done | bytes 442384 | tf_op jit(solution)/shard_map/reduce_scatter | solution.py:361
  217.7 1.9 pad_maximum_fusion
  (11 shorter events, 0.1 us)
Async XLA Ops:
  6.5 3.5 %copy-start.1 = (s32[256]{0:T(256)S(1)}, s32[256]{0:T(256)}, u32[]{:S(2)}) copy-start(s32[256]{0:T(256)} %param.7) | copy-start | bytes 3076
  6.5 3.5 %copy-start = (s32[256]{0:T(256)S(1)}, s32[256]{0:T(256)}, u32[]{:S(2)}) copy-start(s32[256]{0:T(256)} %param.8) | copy-start | bytes 3076
  6.5 131.7 %all-gather.2.cloned.1.call-start = ((), (), s32[]{:S(2)}) async-start(), calls=%async_computation.3 | async-start | bytes 5849088 | tf_op jit(solution)/shard_map/all_gather | solution.py:342
  132.4 47.0 %all-to-all-start.1 = ((bf16[128,8,1536]{2,1,0:T(8,128)(2,1)}), bf16[128,8,1536]{2,1,0:T(8,128)(2,1)}, u32[]{:S(2)}, u32[]{:S(2)}) async-start(bf16[128,8,1536]{2,1,0:T(8,128)(2,1)} %bitcast.8), calls=%async_computation.2 | async-start | bytes 6291456 | tf_op jit(solution)/shard_map/all_to_all | solution.py:351
  138.1 79.6 %reduce-scatter.2.cloned.1.call-start = ((), (), s32[]{:S(2)}) async-start(), calls=%async_computation.4 | async-start | bytes 3981312 | tf_op jit(solution)/shard_map/reduce_scatter | solution.py:361
  191.3 2.7 %collective-permute-start = (bf16[192,2304]{1,0:T(8,128)(2,1)}, bf16[192,2304]{1,0:T(8,128)(2,1)S(1)}, u32[]{:S(2)}, u32[]{:S(2)}) collective-permute-start(bf16[192,2304]{1,0:T(8,128)(2,1)} %get-tuple-element.16), channel_id=1, source_target_pairs={{0,1},{1,0},{2,3},{3,2},{4,5},{5,4},{6,7},{7,6},{8,9},{9,8},{10,11... | collective-permute-start | bytes 2654216 | tf_op jit(solution)/shard_map/ppermute | solution.py:310
  195.5 12.2 %collective-permute-start.1 = (bf16[48,2304]{1,0:T(8,128)(2,1)S(1)}, bf16[48,2304]{1,0:T(8,128)(2,1)S(1)}, u32[]{:S(2)}, u32[]{:S(2)}) collective-permute-start(bf16[48,2304]{1,0:T(8,128)(2,1)S(1)} %get-tuple-element.17), channel_id=1, source_target_pairs={{0,4},{1,5},{2,6},{3,7},{4,0},{5,1},{6,2},{7,3},{8,12},{9,13},{10,... | collective-permute-start | bytes 663560 | tf_op jit(solution)/shard_map/ppermute | solution.py:321
  195.6 16.1 %collective-permute-start.2 = (bf16[48,2304]{1,0:T(8,128)(2,1)S(1)}, bf16[48,2304]{1,0:T(8,128)(2,1)S(1)}, u32[]{:S(2)}, u32[]{:S(2)}) collective-permute-start(bf16[48,2304]{1,0:T(8,128)(2,1)S(1)} %get-tuple-element.19), channel_id=1, source_target_pairs={{0,2},{1,3},{2,4},{3,5},{4,6},{5,7},{6,0},{7,1},{8,10},{9,11},{10,... | collective-permute-start | bytes 663560 | tf_op jit(solution)/shard_map/ppermute | solution.py:321
  196.9 15.2 %collective-permute-start.3 = (bf16[48,2304]{1,0:T(8,128)(2,1)S(1)}, bf16[48,2304]{1,0:T(8,128)(2,1)S(1)}, u32[]{:S(2)}, u32[]{:S(2)}) collective-permute-start(bf16[48,2304]{1,0:T(8,128)(2,1)S(1)} %get-tuple-element.18), channel_id=1, source_target_pairs={{0,6},{1,7},{2,0},{3,1},{4,2},{5,3},{6,4},{7,5},{8,14},{9,15},{10,... | collective-permute-start | bytes 663560 | tf_op jit(solution)/shard_map/ppermute | solution.py:321
Sparse Core Ops, SparseCore 0:
  10.2 119.2 all-gather.1
  171.9 45.7 reduce-scatter.1

commit v6 on v5

--- a/solution.py
+++ b/solution.py
@@ -29,20 +29,28 @@
     return x if amount == 0 else pltpu.roll(x, amount, 1)
 
 
-def pack_kernel(counts, land_ref, lab_ref, low_ref, high_ref, early_ref, late_ref, first, second):
+def pack_kernel(counts, target_ref, k_ref, i_ref, low_ref, high_ref, early_ref, late_ref, first, second):
     step = pl.program_id(0)
     rows = first.shape[0]
 
     @pl.when(step == 0)
     def _():
         row = lax.broadcasted_iota(jnp.int32, first.shape, 0)
-        land = jnp.broadcast_to(land_ref[...], first.shape)
+        held = target_ref.shape[1]
+        across = jnp.broadcast_to(target_ref[...], (held, held))
+        down = jnp.transpose(across)
+        before = lax.broadcasted_iota(jnp.int32, across.shape, 0) < lax.broadcasted_iota(
+            jnp.int32, across.shape, 1
+        )
+        rank = jnp.sum(jnp.where((across == down) & before, 1, 0), axis=0, keepdims=True)
+        land = jnp.broadcast_to(target_ref[...] * SLOTS + rank, first.shape)
         first[...] = jnp.where(row == land, 1.0, 0.0).astype(jnp.bfloat16)
         second[...] = jnp.where((row ^ SLOTS) == land, 1.0, 0.0).astype(jnp.bfloat16)
 
-    def spread(low, high):
-        a = jnp.dot(first[...], low, preferred_element_type=jnp.float32)
-        b = jnp.dot(second[...], high, preferred_element_type=jnp.float32)
+    def spread(low, high, side=0):
+        dims = (((1,), (side,)), ((), ()))
+        a = lax.dot_general(first[...], low, dims, preferred_element_type=jnp.float32)
+        b = lax.dot_general(second[...], high, dims, preferred_element_type=jnp.float32)
         n = a.shape[1]
         a = a.reshape(rows // 8, 1, 8, n)
         b = b.reshape(rows // 8, 1, 8, n)
@@ -56,14 +64,20 @@
 
     @pl.when(step == counts[0])
     def _():
-        early_ref[:, :LANES] = spread(lab_ref[...], lab_ref[...])
+        shape = (LANES, k_ref.shape[1])
+        kind = lax.broadcasted_iota(jnp.int32, shape, 0)
+        k = jnp.broadcast_to(k_ref[...] + 1, shape)
+        i = jnp.broadcast_to(i_ref[...], shape)
+        labels = jnp.where(kind == 0, k, jnp.where(kind == 1, i, 0))
+        labels = labels.astype(jnp.float32).astype(jnp.bfloat16)
+        early_ref[:, :LANES] = spread(labels, labels, 1)
 
     @pl.when(step > counts[0])
     def _():
         late_ref[...] = spread(low_ref[...], high_ref[...])
 
 
-def pack(land, labels, tiles, devices):
+def pack(target, k, i, tiles, devices):
     held = tiles.shape[0]
     block = 768
     counts = [quads * 384 // block for quads in QUADS]
@@ -78,7 +92,8 @@
         ],
         in_specs=[
             pl.BlockSpec((1, held), lambda s: (0, 0)),
-            pl.BlockSpec((held, LANES), lambda s: (0, 0)),
+            pl.BlockSpec((1, held), lambda s: (0, 0)),
+            pl.BlockSpec((1, held), lambda s: (0, 0)),
             pl.BlockSpec((held, block), lambda s: (0, source(s))),
             pl.BlockSpec((held, block), lambda s: (0, HALF // block + source(s))),
         ],
@@ -89,7 +104,7 @@
         scratch_shapes=[pltpu.VMEM((devices * SLOTS, held), jnp.bfloat16)] * 2,
         compiler_params=pltpu.CompilerParams(vmem_limit_bytes=58 * MIB),
         name="pack",
-    )(land, labels, tiles, tiles)
+    )(target[None, :], k[None, :], i[None, :], tiles, tiles)
 
 
 def label_rows(lab):
@@ -324,15 +339,9 @@
     return total.astype(jnp.bfloat16)
 
 
-def lanes_of(columns):
-    stacked = jnp.stack(columns, axis=1).astype(jnp.bfloat16)
-    return jnp.pad(stacked, ((0, 0), (0, LANES - stacked.shape[1])))
-
-
 def on_device(amp_tiles, amp_rows, amp_cols, int_tiles, int_rows, int_cols):
     ctr_count = lax.axis_size("ctr")
     devices = lax.axis_size("pair") * ctr_count
-    held = amp_tiles.shape[0]
     count = int_rows.shape[1]
     square = int_tiles[0].reshape(count, TILE, TILE).transpose(1, 0, 2).reshape(TILE, count * TILE)
     spare = -(-(count * TILE) // LANES) * LANES - count * TILE
@@ -341,12 +350,8 @@
     piece = jnp.concatenate([square, int_labels], axis=1)
     gathered = lax.all_gather(piece, "pair", axis=0, tiled=True)
     target = amp_rows // VT * ctr_count + amp_cols // KT
-    order = jnp.arange(held, dtype=jnp.int32)
-    earlier = (target[:, None] == target[None, :]) & (order[:, None] < order[None, :])
-    land = target * SLOTS + jnp.sum(earlier.astype(jnp.int32), axis=0)
-    labels = lanes_of([amp_cols % KT + 1, amp_rows % VT])
     everyone = ("pair", "ctr")
-    packed = pack(land[None, :], labels, amp_tiles, devices)
+    packed = pack(target, amp_cols % KT, amp_rows % VT, amp_tiles, devices)
     arrived = [
         lax.all_to_all(outgoing, everyone, split_axis=0, concat_axis=0, tiled=True) for outgoing in packed
     ]

time: 228 us -> 228 us (level)
  no operation moved by 1% of the time
where the time goes in v6:
time: 228 us; the launch traced here: 226 us
  blocking collectives  112 us (49%)
  Pallas kernels  53.4 us (23%)
  waiting for transfers between devices  29 us (13%)
  between operations  13.5 us (6%)
  starting transfers between devices  9.25 us (4%)
  other arithmetic  6.96 us (3%)
    all_to_all x1, blocking collectives, on_device(): lax.all_to_all(outgoing, everyone, split_axis=0, concat_axis=0, tiled=True)  112 us
    pallas_call x2, Pallas kernels, product(): pl.pallas_call(functools.partial(product_kernel, depths), grid=(places +...  31.1 us
    ppermute x3, waiting for transfers between devices, sum_depths(): parts.append(lax.ppermute(both[far], 'ctr', move))  13.3 us
    pallas_call x1, Pallas kernels, place_integrals(): pl.pallas_call(integral_kernel, grid=(JT // 4,), out_shape=jax.ShapeDtype...  12.9 us
    pallas_call x1, Pallas kernels, pack(): pl.pallas_call(functools.partial(pack_kernel, counts), grid=(sum(counts)...  9.43 us
    all_to_all x1, waiting for transfers between devices, on_device(): lax.all_to_all(outgoing, everyone, split_axis=0, concat_axis=0, tiled=True)  7.69 us
    all_to_all x1, starting transfers between devices, on_device(): lax.all_to_all(outgoing, everyone, split_axis=0, concat_axis=0, tiled=True)  5.74 us
    reduce_scatter x1, waiting for transfers between devices, on_device(): lax.psum_scatter(value, 'ctr', scatter_dimension=0, tiled=True)  5.36 us
  transfers between devices with their start and end apart: 7, of which 6 were waited for; matrix products, arithmetic and copies ran while one was open for 2% of the time, Pallas kernels for 24%

profile of v6, /device:TPU:0, one launch (start us, length us, event | category | flops | bytes accessed | tf_op | source)
XLA Modules:
  0.0 226.1 jit_solution(1344767367892653525)
XLA Ops:
  6.5 0.0 all-gather.2.cloned.1.call-start
  6.5 1.5 reshape_squeeze.3
  8.0 0.3 copy.8
  8.3 0.2 copy.9
  8.5 0.7 fusion.3
  9.2 0.8 fusion.1
  10.0 0.0 all-gather.2.cloned.1.call-update
  10.0 0.0 copy-done
  10.1 0.6 and_select_fusion.1
  10.6 9.4 %pack.1 = (bf16[1024,3200]{1,0:T(8,128)(2,1)}, bf16[1024,1536]{1,0:T(8,128)(2,1)}) custom-call(s32[1,256]{1,0:T(1,128)} %bitcast.24, s32[1,256]{1,0:T(1,128)} %bitcast.25, s32[1,256]{1,0:T(1,128)} %bitcast.23, bf16[256,9216]{1,0:T(8,128)(2,1)} %high_ref.1, bf16[256,9216]{1,0:T(8,128)(2,1)} %high_ref.1), custom_call_target="tpu_custom_call" | custom-call | tf_op jit(solution)/shard_map/pack/pallas_call | solution.py:86
  20.1 112.0 %all_to_all.23 = bf16[128,8,3200]{2,1,0:T(8,128)(2,1)} all-to-all(bf16[128,8,3200]{2,1,0:T(8,128)(2,1)} %bitcast.18), channel_id=1, replica_groups=mesh['pair'=16,'ctr'=8] {'pair','ctr'}, dimensions={0} | all-to-all | bytes 13107200 | tf_op jit(solution)/shard_map/all_to_all | solution.py:356
  132.1 5.7 %all-to-all-start.1 = ((bf16[128,8,1536]{2,1,0:T(8,128)(2,1)}), bf16[128,8,1536]{2,1,0:T(8,128)(2,1)}, u32[]{:S(2)}, u32[]{:S(2)}) async-start(bf16[128,8,1536]{2,1,0:T(8,128)(2,1)} %bitcast.10), calls=%async_computation.2 | async-start | bytes 6291456 | tf_op jit(solution)/shard_map/all_to_all | solution.py:356
  137.8 0.0 reduce-scatter.2.cloned.1.call-start
  137.9 0.0 all-gather.2.cloned.1.call-done.tiles_hbm
  137.9 1.4 slice_convert_fusion.names_ref
  139.3 12.9 %integrals.1.b_hbm = bf16[2304,2304]{1,0:T(8,128)(2,1)} custom-call(s32[16,2,18]{2,1,0:T(2,128)} %slice_convert_fusion.names_ref, bf16[1536,1792]{1,0:T(8,128)(2,1)} %all-gather.2.cloned.1.call-done.tiles_hbm), custom_call_target="tpu_custom_call" | custom-call | tf_op jit(solution)/shard_map/integrals/pallas_call | solution.py:177
  152.2 19.1 %product.2 = bf16[768,2304]{1,0:T(8,128)(2,1)} custom-call(s32[1]{0:T(128)} %bitcast.ctr_ref, bf16[1024,3200]{1,0:T(8,128)(2,1)} %bitcast.15, bf16[1024,3200]{1,0:T(8,128)(2,1)} %bitcast.16, bf16[2304,2304]{1,0:T(8,128)(2,1)} %integrals.1.b_hbm), custom_call_target="tpu_custom_call" | custom-call | flops 1000000 | bytes 3333 | tf_op jit(solution)/shard_map/product/pallas_call | solution.py:299
  171.4 0.0 reduce-scatter.2.cloned.1.call-update
  171.4 7.7 %all-to-all-done.1 = bf16[128,8,1536]{2,1,0:T(8,128)(2,1)} async-done(((bf16[128,8,1536]{2,1,0:T(8,128)(2,1)}), bf16[128,8,1536]{2,1,0:T(8,128)(2,1)}, u32[]{:S(2)}, u32[]{:S(2)}) %all-to-all-start.1) | async-done | bytes 3145760 | tf_op jit(solution)/shard_map/all_to_all | solution.py:356
  179.1 11.9 %product.3 = (bf16[192,2304]{1,0:T(8,128)(2,1)}, bf16[192,2304]{1,0:T(8,128)(2,1)}) custom-call(s32[1]{0:T(128)} %bitcast.ctr_ref, bf16[1024,3200]{1,0:T(8,128)(2,1)} %bitcast.17, bf16[1024,1536]{1,0:T(8,128)(2,1)} %bitcast.11.tiles_ref, bf16[2304,2304]{1,0:T(8,128)(2,1)} %integrals.1.b_hbm), custom_call_target="tpu_custom_call" | custom-call | flops 99999997952 | bytes 333333344 | tf_op jit(solution)/shard_map/product/pallas_call | solution.py:299
  191.0 0.1 collective-permute-start
  191.1 2.6 %collective-permute-done = bf16[192,2304]{1,0:T(8,128)(2,1)S(1)} collective-permute-done((bf16[192,2304]{1,0:T(8,128)(2,1)}, bf16[192,2304]{1,0:T(8,128)(2,1)S(1)}, u32[]{:S(2)}, u32[]{:S(2)}) %collective-permute-start) | collective-permute-done | bytes 884768 | tf_op jit(solution)/shard_map/ppermute | solution.py:325
  193.7 1.4 add_convert_fusion
  195.2 0.1 collective-permute-start.1
  195.3 1.3 collective-permute-start.2
  196.6 2.0 collective-permute-start.3
  198.6 8.8 %collective-permute-done.1 = bf16[48,2304]{1,0:T(8,128)(2,1)S(1)} collective-permute-done((bf16[48,2304]{1,0:T(8,128)(2,1)S(1)}, bf16[48,2304]{1,0:T(8,128)(2,1)S(1)}, u32[]{:S(2)}, u32[]{:S(2)}) %collective-permute-start.1) | collective-permute-done | bytes 221216 | tf_op jit(solution)/shard_map/ppermute | solution.py:336
  207.4 3.9 %collective-permute-done.2 = bf16[48,2304]{1,0:T(8,128)(2,1)S(1)} collective-permute-done((bf16[48,2304]{1,0:T(8,128)(2,1)S(1)}, bf16[48,2304]{1,0:T(8,128)(2,1)S(1)}, u32[]{:S(2)}, u32[]{:S(2)}) %collective-permute-start.2) | collective-permute-done | bytes 221216 | tf_op jit(solution)/shard_map/ppermute | solution.py:336
  211.3 0.6 collective-permute-done.3
  211.9 0.1 add_convert_fusion.1
  212.0 5.4 %reduce-scatter.2.cloned.1.call-done = bf16[96,2304]{1,0:T(8,128)(2,1)} async-done(((bf16[768,2304]{1,0:T(8,128)(2,1)}), bf16[96,2304]{1,0:T(8,128)(2,1)}) %reduce-scatter.2.cloned.1.call-update) | async-done | bytes 442384 | tf_op jit(solution)/shard_map/reduce_scatter | solution.py:366
  217.4 1.9 pad_maximum_fusion
  (4 shorter events, 0.1 us)
Async XLA Ops:
  6.5 3.5 %copy-start = (s32[256]{0:T(256)S(1)}, s32[256]{0:T(256)}, u32[]{:S(2)}) copy-start(s32[256]{0:T(256)} %param.7) | copy-start | bytes 3076
  6.5 3.5 %copy-start.1 = (s32[256]{0:T(256)S(1)}, s32[256]{0:T(256)}, u32[]{:S(2)}) copy-start(s32[256]{0:T(256)} %param.8) | copy-start | bytes 3076
  6.5 131.3 %all-gather.2.cloned.1.call-start = ((), (), s32[]{:S(2)}) async-start(), calls=%async_computation.3 | async-start | bytes 5849088 | tf_op jit(solution)/shard_map/all_gather | solution.py:351
  132.1 47.0 %all-to-all-start.1 = ((bf16[128,8,1536]{2,1,0:T(8,128)(2,1)}), bf16[128,8,1536]{2,1,0:T(8,128)(2,1)}, u32[]{:S(2)}, u32[]{:S(2)}) async-start(bf16[128,8,1536]{2,1,0:T(8,128)(2,1)} %bitcast.10), calls=%async_computation.2 | async-start | bytes 6291456 | tf_op jit(solution)/shard_map/all_to_all | solution.py:356
  137.8 79.6 %reduce-scatter.2.cloned.1.call-start = ((), (), s32[]{:S(2)}) async-start(), calls=%async_computation.4 | async-start | bytes 3981312 | tf_op jit(solution)/shard_map/reduce_scatter | solution.py:366
  191.0 2.7 %collective-permute-start = (bf16[192,2304]{1,0:T(8,128)(2,1)}, bf16[192,2304]{1,0:T(8,128)(2,1)S(1)}, u32[]{:S(2)}, u32[]{:S(2)}) collective-permute-start(bf16[192,2304]{1,0:T(8,128)(2,1)} %get-tuple-element.16), channel_id=1, source_target_pairs={{0,1},{1,0},{2,3},{3,2},{4,5},{5,4},{6,7},{7,6},{8,9},{9,8},{10,11... | collective-permute-start | bytes 2654216 | tf_op jit(solution)/shard_map/ppermute | solution.py:325
  195.2 12.2 %collective-permute-start.1 = (bf16[48,2304]{1,0:T(8,128)(2,1)S(1)}, bf16[48,2304]{1,0:T(8,128)(2,1)S(1)}, u32[]{:S(2)}, u32[]{:S(2)}) collective-permute-start(bf16[48,2304]{1,0:T(8,128)(2,1)S(1)} %get-tuple-element.17), channel_id=1, source_target_pairs={{0,4},{1,5},{2,6},{3,7},{4,0},{5,1},{6,2},{7,3},{8,12},{9,13},{10,... | collective-permute-start | bytes 663560 | tf_op jit(solution)/shard_map/ppermute | solution.py:336
  195.3 16.0 %collective-permute-start.2 = (bf16[48,2304]{1,0:T(8,128)(2,1)S(1)}, bf16[48,2304]{1,0:T(8,128)(2,1)S(1)}, u32[]{:S(2)}, u32[]{:S(2)}) collective-permute-start(bf16[48,2304]{1,0:T(8,128)(2,1)S(1)} %get-tuple-element.19), channel_id=1, source_target_pairs={{0,2},{1,3},{2,4},{3,5},{4,6},{5,7},{6,0},{7,1},{8,10},{9,11},{10,... | collective-permute-start | bytes 663560 | tf_op jit(solution)/shard_map/ppermute | solution.py:336
  196.6 15.3 %collective-permute-start.3 = (bf16[48,2304]{1,0:T(8,128)(2,1)S(1)}, bf16[48,2304]{1,0:T(8,128)(2,1)S(1)}, u32[]{:S(2)}, u32[]{:S(2)}) collective-permute-start(bf16[48,2304]{1,0:T(8,128)(2,1)S(1)} %get-tuple-element.18), channel_id=1, source_target_pairs={{0,6},{1,7},{2,0},{3,1},{4,2},{5,3},{6,4},{7,5},{8,14},{9,15},{10,... | collective-permute-start | bytes 663560 | tf_op jit(solution)/shard_map/ppermute | solution.py:336
Sparse Core Ops, SparseCore 0:
  10.2 117.7 all-gather.1
  171.5 45.7 reduce-scatter.1
